TPU v7x, 1024 devices: a whole 4x8x16 slice. The times are simulated.
1024 devices in a mesh: dp: 64 (over y, x, z_hi), group: 16 (over z_lo, core).
Axes of the slice: x: 4, y: 8, z: 16 (z_hi: 2, z_lo: 8; z = z_hi * 8 + z_lo), core: 2. Of those that a mesh axis runs over, the one named last changes fastest.
Arguments:
- images: bfloat16 [12288, 1152], P(('dp', 'group')), may hold values from -0.29882812 to 0.29882812
- texts: bfloat16 [12288, 1152], P(('dp', 'group')), may hold values from -0.29882812 to 0.29882812
- log_scale: float32 [1], replicated, may hold values from 2.3 to 3.4
- bias: float32 [1], replicated, may hold values from -5 to -2
Outputs:
- image_grad: float32 [12288, 1152], P(('dp', 'group'))
- text_grad: float32 [12288, 1152], P(('dp', 'group'))
- statistics: float32 [2], replicated
All inputs are finite; a program needn't handle non-finite values.
Results may differ from a plain program's by a relative error of at most 0.002.
The roundings to bfloat16 on the way count: a program that leaves them out, or rounds other values in their place, can miss the bound.
Values may be sent and summed in bfloat16 or wider, within the bound.
A program may use at most 32 MiB of HBM per device.

v0:
```python
import jax
import jax.numpy as jnp
from jax import lax
from jax.sharding import PartitionSpec as P


def unit_rows(values):
    full = values.astype(jnp.float32)
    inverse = lax.rsqrt(jnp.sum(full * full, axis=1, keepdims=True) + 1e-06)
    return (full * inverse, inverse)


def back_unit(unit, inverse, grad):
    return (grad - unit * jnp.sum(unit * grad, axis=1, keepdims=True)) * inverse


def pair_weights(left, right, left_ids, right_ids, scale, shift):
    cosine = jnp.dot(left, right.T, preferred_element_type=jnp.float32)
    logit = scale * cosine + shift
    sign = jnp.where(left_ids[:, None] == right_ids[None, :], 1.0, -1.0).astype(jnp.float32)
    weight = -sign * jax.nn.sigmoid(-sign * logit)
    weight_b = weight.astype(jnp.bfloat16)
    sums = (jnp.sum(weight * scale * cosine), jnp.sum(weight))
    return (weight_b, sums)


def shards(images, texts, log_scale, bias):
    rows = images.shape[0]
    img_unit, inv_img = unit_rows(images)
    txt_unit, inv_txt = unit_rows(texts)
    img_b = img_unit.astype(jnp.bfloat16)
    txt_b = txt_unit.astype(jnp.bfloat16)
    n_wide = lax.axis_size("dp")
    n_narrow = lax.axis_size("group")
    wide_pos = lax.axis_index("dp")
    narrow_pos = lax.axis_index("group")
    scale = jnp.exp(log_scale[0])
    shift = bias[0]
    left = lax.all_gather(img_b, "group", axis=0, tiled=True)
    left_ids = wide_pos * n_narrow * rows + jnp.arange(n_narrow * rows, dtype=jnp.int32)
    right = lax.all_gather(txt_b, "dp", axis=0, tiled=True)
    right_ids = ((jnp.arange(n_wide, dtype=jnp.int32) * n_narrow + narrow_pos) * rows)[
        :, None
    ] + jnp.arange(rows, dtype=jnp.int32)[None, :]
    right_ids = right_ids.reshape(-1)
    weight_b, partial_sums = pair_weights(left, right, left_ids, right_ids, scale, shift)
    picked = weight_b
    txt_unit_grad = lax.psum_scatter(
        scale
        * lax.dot_general(
            picked, left, (((0,), (0,)), ((), ())), preferred_element_type=jnp.float32
        ),
        "dp",
        scatter_dimension=0,
        tiled=True,
    )
    picked = weight_b
    img_unit_grad = lax.psum_scatter(
        scale * jnp.dot(picked, right, preferred_element_type=jnp.float32),
        "group",
        scatter_dimension=0,
        tiled=True,
    )
    scale_sum, bias_sum = lax.psum((partial_sums[0], partial_sums[1]), ("dp", "group"))
    statistics = jnp.stack([scale_sum, bias_sum])
    image_grad = back_unit(img_unit, inv_img, img_unit_grad)
    text_grad = back_unit(txt_unit, inv_txt, txt_unit_grad)
    return (image_grad, text_grad, statistics)


def solution(mesh):
    in_specs = (P(("dp", "group"), None), P(("dp", "group"), None), P(), P())
    out_specs = (P(("dp", "group"), None), P(("dp", "group"), None), P())
    return jax.shard_map(shards, mesh=mesh, in_specs=in_specs, out_specs=out_specs, check_vma=False)
```

profile of v0, /device:TPU:1, one launch (start us, length us, event | category | flops | bytes accessed | tf_op | source)
XLA Modules:
  0.0 1078.3 jit_solution(10591837956335662287)
XLA Ops:
  8.1 1.5 fusion.19
  12.9 43.7 %all-gather = bf16[16,12,1152]{2,1,0:T(8,128)(2,1)S(1)} all-gather(bf16[1,12,1152]{2,1,0:T(8,128)(2,1)S(1)} %fusion.18), channel_id=1, replica_groups=mesh['dp'=64,'group'=16] {'group'}, dimensions={0}, use_global_device_ids=true | all-gather | bytes 470016 | tf_op jit(solution)/shard_map/all_gather | solution.py:39
  56.7 145.5 %all-gather.4.cloned.1.call-done = bf16[64,12,1152]{2,1,0:T(8,128)(2,1)} async-done(((bf16[1,12,1152]{2,1,0:T(8,128)(2,1)}), bf16[64,12,1152]{2,1,0:T(8,128)(2,1)}) %all-gather.4.cloned.1.call-update) | async-done | bytes 1769488 | tf_op jit(solution)/shard_map/all_gather | solution.py:41
  202.2 2.5 reshape.48
  204.8 1.5 multiply_reduce_fusion
  207.1 55.3 %fusion = f32[16,1152]{1,0:T(8,128)} fusion(f32[192,1152]{1,0:T(8,128)S(1)} %convolution_multiply_fusion.1), kind=kCustom, calls=%all-reduce-scatter | all-reduce-scatter fusion | flops 294913 | bytes 962560
  262.4 1.5 slice
  263.9 1.9 collective-permute-start.2
  265.8 1.9 collective-permute-start.1
  267.7 1.9 collective-permute-start
  269.6 1.9 collective-permute-start.3
  271.6 2.1 convolution_multiply_fusion
  273.7 550.2 %fusion.1 = f32[16,1152]{1,0:T(8,128)} fusion(f32[768,1152]{1,0:T(8,128)S(1)} %convolution_multiply_fusion), kind=kCustom, calls=%all-reduce-scatter.1 | all-reduce-scatter fusion | flops 1179649 | bytes 3616768
  826.1 1.4 dynamic-slice.10
  830.1 149.8 %all-reduce.4 = (f32[1]{0:T(128)}, f32[1]{0:T(128)}) all-reduce(f32[1]{0:T(128)} %bitcast.5, f32[1]{0:T(128)} %bitcast.4), channel_id=1, replica_groups=mesh['dp'=64,'group'=16] {'dp','group'}, use_global_device_ids=true, to_apply=%region_9.10 | all-reduce | flops 2 | bytes 16 | tf_op jit(solution)/shard_map/psum | solution.py:64
  979.9 8.6 collective-permute-start.18
  988.5 7.0 collective-permute-start.17
  995.5 10.1 collective-permute-start.16
  1005.6 1.4 collective-permute-start.15
  1007.0 7.9 collective-permute-start.14
  1014.9 1.8 pad_maximum_fusion
  1016.7 4.8 concatenate
  1021.5 1.3 collective-permute-start.13
  1022.9 4.1 collective-permute-start.12
  1028.3 10.0 collective-permute-start.10
  1038.4 1.5 collective-permute-start.9
  1040.9 3.2 collective-permute-start.8
  1044.2 4.7 collective-permute-start.7
  1048.9 8.4 collective-permute-start.6
  1058.6 7.2 collective-permute-start.4
  1065.7 1.5 fusion.12
  1067.4 3.1 concatenate.1
  (47 shorter events, 11.9 us)
Async XLA Ops:
  7.2 195.0 %all-gather.4.cloned.1.call-start = ((), (), s32[]{:S(2)}) async-start(), calls=%async_computation | async-start | bytes 2396160 | tf_op jit(solution)/shard_map/all_gather | solution.py:41
  56.7 148.0 %copy-start.1 = (bf16[192,1152]{1,0:T(8,128)(2,1)}, bf16[192,1152]{1,0:T(8,128)(2,1)S(1)}, u32[]{:S(2)}) copy-start(bf16[192,1152]{1,0:T(8,128)(2,1)S(1)} %reshape.46) | copy-start | bytes 1327108
  206.2 0.8 copy-start.2
  263.9 731.6 %collective-permute-start.2 = (f32[16,1152]{1,0:T(8,128)}, f32[16,1152]{1,0:T(8,128)}, u32[]{:S(2)}, u32[]{:S(2)}) collective-permute-start(f32[16,1152]{1,0:T(8,128)} %fusion), channel_id=1, source_target_pairs={{0,3},{1,4},{2,5},{3,6},{4,7},{5,8},{6,9},{7,10},{8,11},{9,12},{10... | collective-permute-start | bytes 221192
  265.8 739.8 %collective-permute-start.1 = (f32[16,1152]{1,0:T(8,128)}, f32[16,1152]{1,0:T(8,128)}, u32[]{:S(2)}, u32[]{:S(2)}) collective-permute-start(f32[16,1152]{1,0:T(8,128)} %fusion), channel_id=1, source_target_pairs={{0,2},{1,3},{2,4},{3,5},{4,6},{5,7},{6,8},{7,9},{8,10},{9,11},{10,... | collective-permute-start | bytes 221192
  267.7 739.2 %collective-permute-start = (f32[16,1152]{1,0:T(8,128)}, f32[16,1152]{1,0:T(8,128)}, u32[]{:S(2)}, u32[]{:S(2)}) collective-permute-start(f32[16,1152]{1,0:T(8,128)} %fusion), channel_id=1, source_target_pairs={{0,1},{1,2},{2,3},{3,4},{4,5},{5,6},{6,7},{7,8},{8,9},{9,10},{10,1... | collective-permute-start | bytes 221192
  269.6 710.3 %collective-permute-start.3 = (f32[12,1152]{1,0:T(8,128)}, f32[12,1152]{1,0:T(8,128)}, u32[]{:S(2)}, u32[]{:S(2)}) collective-permute-start(f32[12,1152]{1,0:T(8,128)} %slice), channel_id=1, source_target_pairs={{0,4},{1,5},{2,6},{3,7},{4,8},{5,9},{6,10},{7,11},{8,12},{9,13},{1... | collective-permute-start | bytes 165896
  824.8 163.7 %collective-permute-start.19 = (f32[12,1152]{1,0:T(8,128)S(1)}, f32[12,1152]{1,0:T(8,128)S(1)}, u32[]{:S(2)}, u32[]{:S(2)}) collective-permute-start(f32[12,1152]{1,0:T(8,128)S(1)} %slice.1), channel_id=1, source_target_pairs={{0,256},{16,272},{32,288},{48,304},{64,320},{80,336},{96,352},{112... | collective-permute-start | bytes 165896
  979.9 41.6 %collective-permute-start.18 = (f32[16,1152]{1,0:T(8,128)}, f32[16,1152]{1,0:T(8,128)S(1)}, u32[]{:S(2)}, u32[]{:S(2)}) collective-permute-start(f32[16,1152]{1,0:T(8,128)} %fusion.1), channel_id=1, source_target_pairs={{0,240},{16,256},{32,272},{48,288},{64,304},{80,320},{96,336},{112... | collective-permute-start | bytes 221192
  988.5 34.4 %collective-permute-start.17 = (f32[16,1152]{1,0:T(8,128)}, f32[16,1152]{1,0:T(8,128)S(1)}, u32[]{:S(2)}, u32[]{:S(2)}) collective-permute-start(f32[16,1152]{1,0:T(8,128)} %fusion.1), channel_id=1, source_target_pairs={{0,224},{16,240},{32,256},{48,272},{64,288},{80,304},{96,320},{112... | collective-permute-start | bytes 221192
  995.5 31.5 %collective-permute-start.16 = (f32[16,1152]{1,0:T(8,128)}, f32[16,1152]{1,0:T(8,128)S(1)}, u32[]{:S(2)}, u32[]{:S(2)}) collective-permute-start(f32[16,1152]{1,0:T(8,128)} %fusion.1), channel_id=1, source_target_pairs={{0,208},{16,224},{32,240},{48,256},{64,272},{80,288},{96,304},{112... | collective-permute-start | bytes 221192
  1005.6 22.7 %collective-permute-start.15 = (f32[16,1152]{1,0:T(8,128)}, f32[16,1152]{1,0:T(8,128)S(1)}, u32[]{:S(2)}, u32[]{:S(2)}) collective-permute-start(f32[16,1152]{1,0:T(8,128)} %fusion.1), channel_id=1, source_target_pairs={{0,192},{16,208},{32,224},{48,240},{64,256},{80,272},{96,288},{112... | collective-permute-start | bytes 221192
  1007.0 31.4 %collective-permute-start.14 = (f32[16,1152]{1,0:T(8,128)}, f32[16,1152]{1,0:T(8,128)S(1)}, u32[]{:S(2)}, u32[]{:S(2)}) collective-permute-start(f32[16,1152]{1,0:T(8,128)} %fusion.1), channel_id=1, source_target_pairs={{0,176},{16,192},{32,208},{48,224},{64,240},{80,256},{96,272},{112... | collective-permute-start | bytes 221192
  1016.7 53.8 %copy-start = (bf16[12,1152]{1,0:T(8,128)(2,1)S(1)}, bf16[12,1152]{1,0:T(8,128)(2,1)}, u32[]{:S(2)}) copy-start(bf16[12,1152]{1,0:T(8,128)(2,1)} %param.5) | copy-start | bytes 82948
  1021.5 19.3 %collective-permute-start.13 = (f32[16,1152]{1,0:T(8,128)}, f32[16,1152]{1,0:T(8,128)S(1)}, u32[]{:S(2)}, u32[]{:S(2)}) collective-permute-start(f32[16,1152]{1,0:T(8,128)} %fusion.1), channel_id=1, source_target_pairs={{0,160},{16,176},{32,192},{48,208},{64,224},{80,240},{96,256},{112... | collective-permute-start | bytes 221192
  1022.9 21.3 %collective-permute-start.12 = (f32[16,1152]{1,0:T(8,128)}, f32[16,1152]{1,0:T(8,128)S(1)}, u32[]{:S(2)}, u32[]{:S(2)}) collective-permute-start(f32[16,1152]{1,0:T(8,128)} %fusion.1), channel_id=1, source_target_pairs={{0,144},{16,160},{32,176},{48,192},{64,208},{80,224},{96,240},{112... | collective-permute-start | bytes 221192
  1027.0 21.9 %collective-permute-start.11 = (f32[16,1152]{1,0:T(8,128)}, f32[16,1152]{1,0:T(8,128)S(1)}, u32[]{:S(2)}, u32[]{:S(2)}) collective-permute-start(f32[16,1152]{1,0:T(8,128)} %fusion.1), channel_id=1, source_target_pairs={{0,128},{16,144},{32,160},{48,176},{64,192},{80,208},{96,224},{112... | collective-permute-start | bytes 221192
  1028.3 28.9 %collective-permute-start.10 = (f32[16,1152]{1,0:T(8,128)}, f32[16,1152]{1,0:T(8,128)S(1)}, u32[]{:S(2)}, u32[]{:S(2)}) collective-permute-start(f32[16,1152]{1,0:T(8,128)} %fusion.1), channel_id=1, source_target_pairs={{0,112},{16,128},{32,144},{48,160},{64,176},{80,192},{96,208},{112... | collective-permute-start | bytes 221192
  1038.4 20.2 %collective-permute-start.9 = (f32[16,1152]{1,0:T(8,128)}, f32[16,1152]{1,0:T(8,128)S(1)}, u32[]{:S(2)}, u32[]{:S(2)}) collective-permute-start(f32[16,1152]{1,0:T(8,128)} %fusion.1), channel_id=1, source_target_pairs={{0,96},{16,112},{32,128},{48,144},{64,160},{80,176},{96,192},{112,... | collective-permute-start | bytes 221192
  1040.9 26.3 %collective-permute-start.8 = (f32[16,1152]{1,0:T(8,128)}, f32[16,1152]{1,0:T(8,128)S(1)}, u32[]{:S(2)}, u32[]{:S(2)}) collective-permute-start(f32[16,1152]{1,0:T(8,128)} %fusion.1), channel_id=1, source_target_pairs={{0,80},{16,96},{32,112},{48,128},{64,144},{80,160},{96,176},{112,1... | collective-permute-start | bytes 221192
  1044.2 23.1 %collective-permute-start.7 = (f32[16,1152]{1,0:T(8,128)}, f32[16,1152]{1,0:T(8,128)S(1)}, u32[]{:S(2)}, u32[]{:S(2)}) collective-permute-start(f32[16,1152]{1,0:T(8,128)} %fusion.1), channel_id=1, source_target_pairs={{0,64},{16,80},{32,96},{48,112},{64,128},{80,144},{96,160},{112,17... | collective-permute-start | bytes 221192
  1048.9 18.4 %collective-permute-start.6 = (f32[16,1152]{1,0:T(8,128)}, f32[16,1152]{1,0:T(8,128)S(1)}, u32[]{:S(2)}, u32[]{:S(2)}) collective-permute-start(f32[16,1152]{1,0:T(8,128)} %fusion.1), channel_id=1, source_target_pairs={{0,48},{16,64},{32,80},{48,96},{64,112},{80,128},{96,144},{112,160... | collective-permute-start | bytes 221192
  1057.2 10.0 collective-permute-start.5
  1058.6 8.9 collective-permute-start.4
Sparse Core Ops, SparseCore 0:
  14.4 187.7 all-gather.3
where the time goes:
time: 1090 us; the launch traced here: 1080 us
  blocking collectives  799 us (73%)
  waiting for transfers between devices  146 us (13%)
  starting transfers between devices  87 us (8%)
  between operations  17.1 us (2%)
  local copies, waits for them, and re-layouts  15.7 us (1%)
    unnamed x2, blocking collectives  606 us
    psum x1, blocking collectives, shards(): lax.psum((partial_sums[0], partial_sums[1]), ('dp', 'group'))  150 us
    all_gather x1, waiting for transfers between devices, shards(): right = lax.all_gather(txt_b, 'dp', axis=0, tiled=True)  145 us
    unnamed x20, starting transfers between devices  86.9 us
    all_gather x1, blocking collectives, shards(): left = lax.all_gather(img_b, 'group', axis=0, tiled=True)  43.7 us
  transfers between devices with their start and end apart: 21, of which 2 were waited for; matrix products, arithmetic and copies ran while one was open for 53% of the time, Pallas kernels for 0%

commit v1 on v0

v1 whole, which is shorter than its diff:
```python
import jax
import jax.numpy as jnp
from jax import lax
from jax.experimental import pallas as pl
from jax.experimental.pallas import tpu as pltpu
from jax.sharding import PartitionSpec as P

D = 1152
ROWS = 12
PAD = 16
X, Y, Z = 4, 8, 16
Y_OFF = (0, 1, -1, 2, -2, 3, -3, 4)
Z_NEAR = (0, -1, 1, -2)
Z_FAR = (0, 4, -4, 8)
NX, NY, NN, NF = len(range(X)), len(Y_OFF), len(Z_NEAR), len(Z_FAR)
L_OWN = NN * NF * PAD
R_OWN = NX * NY * PAD
COLUMNS = ((0, 384), (384, 384), (768, 384))
NC = len(COLUMNS)
Y_GROUPS = ((0, 1), (1, 3), (3, 5), (5, 8))
F_GROUPS = ((0, 1), (1, 3), (3, 4))
MESH = pl.DeviceIdType.MESH
F32, BF16 = jnp.float32, jnp.bfloat16


def slot(offsets, size, offset):
    return [o % size for o in offsets].index(offset % size)


def kernel(
    img_ref, txt_ref, ls_ref, bias_ref, ig_ref, tg_ref, st_ref,
    lall, rall, cosb, wt, wb, tp, tx, ty, ip, iz, iw, stat, stat_in, send_sem, recv_sem,
):
    dp, group = lax.axis_index("dp"), lax.axis_index("group")
    zh, xx, yy = dp % 2, (dp // 2) % X, dp // (2 * X)
    zz, cc = zh * 8 + group // 2, group % 2

    def at(dx=0, dy=0, dz=0, dc=0):
        x, y, z, c = (xx + dx + X) % X, (yy + dy + Y) % Y, (zz + dz + Z) % Z, (cc + dc) % 2
        return ((y * X + x) * 2 + z // 8, (z % 8) * 2 + c)

    partners = [at(dx=d) for d in range(1, X)] + [at(dy=d) for d in Y_OFF[1:]]
    partners += [at(dz=d) for d in (1, -1, 2, -2, 4, -4, 8)] + [at(dc=1)]
    barrier = pltpu.get_barrier_semaphore()
    for p in partners:
        pl.semaphore_signal(barrier, inc=1, device_id=p, device_id_type=MESH)

    copies = []

    def send(src, dst, device):
        k = len(copies)
        copy = pltpu.make_async_remote_copy(
            src_ref=src, dst_ref=dst, send_sem=send_sem.at[k], recv_sem=recv_sem.at[k],
            device_id=device, device_id_type=MESH,
        )
        copy.start()
        copies.append(copy)
        return copy

    def unit(ref):
        full = ref[...].astype(F32)
        inverse = lax.rsqrt(jnp.sum(full * full, axis=1, keepdims=True) + 1e-06)
        return full * inverse, inverse

    for ref, own in ((img_ref, lall.at[0, 0, 0]), (txt_ref, rall.at[0, 0, 0])):
        own[...] = jnp.zeros((PAD, D), BF16)
        own[0:ROWS, :] = unit(ref)[0].astype(BF16)
    pl.semaphore_wait(barrier, len(partners))

    z_far = {}
    for f in (3, 1, 2):
        z_far[f] = send(lall.at[0, 0, 0], lall.at[0, 0, slot(Z_FAR, Z, -Z_FAR[f])], at(dz=Z_FAR[f]))
    y_got = {}
    for j in (7, 5, 6, 3, 4, 1, 2):
        to = slot(Y_OFF, Y, -Y_OFF[j])
        y_got[to] = send(rall.at[0, 0, 0], rall.at[0, 0, to], at(dy=Y_OFF[j]))
    x_got, n_got = [], []

    def x_send(lo, hi):
        for d in (2, 1, 3):
            part = pl.ds(lo, hi - lo)
            x_got.append(send(rall.at[0, 0, part], rall.at[0, X - d, part], at(dx=d)))

    def n_send(lo, hi):
        for n in (3, 1, 2):
            part = pl.ds(lo, hi - lo)
            n_got.append(send(lall.at[0, 0, part], lall.at[0, n, part], at(dz=-Z_NEAR[n])))

    far_slot = {slot(Z_FAR, Z, -Z_FAR[f]): z_far[f] for f in z_far}
    n_send(0, 1)
    x_send(0, 1)
    for lo, hi in Y_GROUPS[1:3]:
        for j in range(lo, hi):
            y_got[j].wait_recv()
        x_send(lo, hi)
    for f in (1, 2):
        far_slot[f].wait_recv()
    n_send(1, 3)
    for j in range(5, 8):
        y_got[j].wait_recv()
    x_send(5, 8)
    shared = [send(rall.at[0, 0], rall.at[1, 0], at(dc=1))]
    far_slot[3].wait_recv()
    n_send(3, 4)
    shared.append(send(lall.at[0, 0], lall.at[1, 0], at(dc=1)))
    for i, d in enumerate((2, 1, 3)):
        for copy in x_got[i::3]:
            copy.wait_recv()
        shared.append(send(rall.at[0, X - d], rall.at[1, X - d], at(dc=1)))
    for i, n in enumerate((3, 1, 2)):
        for copy in n_got[i::3]:
            copy.wait_recv()
        shared.append(send(lall.at[0, n], lall.at[1, n], at(dc=1)))
    for copy in shared:
        copy.wait_recv()

    scale = jnp.exp(jnp.full((1, 1), ls_ref[0], F32))
    shift = jnp.full((1, 1), bias_ref[0], F32)
    dims = (((1,), (1,)), ((), ()))

    def sigmoid(logit):
        return 1.0 / (1.0 + jnp.exp(-logit))

    left = lall.reshape(2 * L_OWN, D)
    right = rall.reshape(2 * R_OWN, D)
    cosb[...] = lax.dot_general(right[0:R_OWN, :], left[...], dims, preferred_element_type=F32)
    step = 64
    row_ok = lax.broadcasted_iota(jnp.int32, (step, 2 * L_OWN), 0) % PAD < ROWS
    col_ok = lax.broadcasted_iota(jnp.int32, (step, 2 * L_OWN), 1) % PAD < ROWS
    ok = jnp.where(row_ok & col_ok, 1.0, 0.0).astype(F32)

    def fold(a):
        return jnp.sum(a.reshape(step // 8, 8, a.shape[1]), axis=0)

    def weigh(i, sums):
        part = pl.ds(pl.multiple_of(i * step, step), step)
        cosine = cosb[part, :]
        weight = sigmoid(scale * cosine + shift)
        wt[part, :] = weight.astype(BF16)
        return sums[0] + fold(weight * cosine), sums[1] + fold(weight * ok)

    zero = jnp.zeros((8, 2 * L_OWN), F32)
    sum_scale, sum_bias = lax.fori_loop(0, R_OWN // step, weigh, (zero, zero))

    def lanes(a):
        return sum(a[:, 128 * i : 128 * (i + 1)] for i in range(a.shape[1] // 128))

    rows16 = lax.broadcasted_iota(jnp.int32, (PAD, 128), 0)
    cols16 = lax.broadcasted_iota(jnp.int32, (PAD, 128), 1)
    diagonal = rows16 == cols16
    counted = jnp.where(diagonal & (rows16 < ROWS), 1.0, 0.0).astype(F32)
    cosine = cosb[0:PAD, 0:128]
    logit = scale * cosine + shift
    other = sigmoid(logit)
    same = -sigmoid(-logit)
    wt[0:PAD, 0:128] = jnp.where(diagonal, same, other).astype(BF16)
    change = (same - other) * counted
    change_scale = change * cosine
    stat[0, 0:8, :] = (lanes(sum_scale) + change_scale[0:8] + change_scale[8:16]) * scale
    stat[0, 8:16, :] = lanes(sum_bias) + change[0:8] + change[8:16]

    def stat_send(level, devices):
        return [send(stat.at[level], stat_in.at[level, i], d) for i, d in enumerate(devices)]

    def stat_take(level, got):
        total = stat[level]
        for i, copy in enumerate(got):
            copy.wait_recv()
            total += stat_in[level, i]
        stat[level + 1] = total

    got0 = stat_send(0, [at(dz=d) for d in Z_NEAR[1:]])

    half = 2 * R_OWN // 2
    for h in range(2):
        cosb[0:L_OWN, :] = lax.dot_general(
            left[0:L_OWN, :], right[h * half : (h + 1) * half, :], dims, preferred_element_type=F32
        )

        def weigh_b(i, carry):
            part = pl.ds(pl.multiple_of(i * step, step), step)
            wb[part, h * half : (h + 1) * half] = sigmoid(scale * cosb[part, :] + shift).astype(BF16)
            return carry

        lax.fori_loop(0, L_OWN // step, weigh_b, 0)
        if h == 0:
            logit = scale * cosb[0:PAD, 0:128] + shift
            wb[0:PAD, 0:128] = jnp.where(diagonal, -sigmoid(-logit), sigmoid(logit)).astype(BF16)

    x_in, n_in = [], []
    for k, (begin, width) in enumerate(COLUMNS):
        cols = pl.ds(begin, width)
        t = jnp.dot(wt[...], left[:, cols], preferred_element_type=F32)
        tp[k] = t.reshape(NX, NY, PAD, width)[:, :, 0:ROWS, :]
        x_in.append({d: send(tp.at[k, d], tx.at[k, d - 1], at(dx=d)) for d in (2, 1, 3)})
        m = jnp.dot(wb[...], right[:, cols], preferred_element_type=F32)
        ip[k] = m.reshape(NN, NF, PAD, width)[:, :, 0:ROWS, :]
        n_in.append({n: send(ip.at[k, n], iz.at[k, n - 1], at(dz=Z_NEAR[n])) for n in (3, 1, 2)})
    stat_take(0, got0)
    got1 = stat_send(1, [at(dz=d) for d in Z_FAR[1:]])
    f_in, y_in = [], []
    for k in range(NC):
        for n in (1, 2, 3):
            n_in[k][n].wait_recv()
        ip[k, 0] += iz[k, 0] + iz[k, 1] + iz[k, 2]
        f_in.append([send(ip.at[k, 0, f], iw.at[k, f - 1], at(dz=Z_FAR[f])) for f in (3, 1, 2)])
        for d in (1, 3, 2):
            x_in[k][d].wait_recv()
        tp[k, 0] += tx[k, 0] + tx[k, 1] + tx[k, 2]
        y_in.append([send(tp.at[k, 0, j], ty.at[k, j - 1], at(dy=Y_OFF[j])) for j in (7, 5, 6, 3, 4, 1, 2)])
        if k == 1:
            stat_take(1, got1)
            got2 = stat_send(2, [at(dx=d) for d in range(1, X)])
    stat_take(2, got2)
    got3 = stat_send(3, [at(dy=d) for d in Y_OFF[1:]])

    def back(ref, total, out_ref):
        u, inverse = unit(ref)
        grad = scale * total
        out_ref[...] = (grad - u * jnp.sum(u * grad, axis=1, keepdims=True)) * inverse

    for k in range(NC):
        for copy in f_in[k]:
            copy.wait_recv()
    parts = [ip[k, 0, 0] + iw[k, 0] + iw[k, 1] + iw[k, 2] for k in range(NC)]
    back(img_ref, jnp.concatenate(parts, axis=1), ig_ref)
    stat_take(3, got3)
    got4 = stat_send(4, [at(dc=1)])
    for k in range(NC):
        for copy in y_in[k]:
            copy.wait_recv()
    parts = []
    for k in range(NC):
        total = tp[k, 0, 0]
        for j in range(NY - 1):
            total += ty[k, j]
        parts.append(total)
    back(txt_ref, jnp.concatenate(parts, axis=1), tg_ref)
    stat_take(4, got4)
    st_ref[0] = jnp.sum(stat[5, 0:8, :])
    st_ref[1] = jnp.sum(stat[5, 8:16, :])
    for copy in copies:
        copy.wait_send()


N_COPIES = 192


def shards(images, texts, log_scale, bias):
    width = COLUMNS[0][1]
    vmem, smem = pl.BlockSpec(memory_space=pltpu.VMEM), pl.BlockSpec(memory_space=pltpu.SMEM)
    return pl.pallas_call(
        kernel,
        out_shape=(
            jax.ShapeDtypeStruct((ROWS, D), F32),
            jax.ShapeDtypeStruct((ROWS, D), F32),
            jax.ShapeDtypeStruct((2,), F32),
        ),
        in_specs=[vmem, vmem, smem, smem],
        out_specs=(vmem, vmem, smem),
        scratch_shapes=[
            pltpu.VMEM((2, NN, NF, PAD, D), BF16),
            pltpu.VMEM((2, NX, NY, PAD, D), BF16),
            pltpu.VMEM((R_OWN, 2 * L_OWN), F32),
            pltpu.VMEM((R_OWN, 2 * L_OWN), BF16),
            pltpu.VMEM((L_OWN, 2 * R_OWN), BF16),
            pltpu.VMEM((NC, NX, NY, ROWS, width), F32),
            pltpu.VMEM((NC, NX - 1, NY, ROWS, width), F32),
            pltpu.VMEM((NC, NY - 1, ROWS, width), F32),
            pltpu.VMEM((NC, NN, NF, ROWS, width), F32),
            pltpu.VMEM((NC, NN - 1, NF, ROWS, width), F32),
            pltpu.VMEM((NC, NF - 1, ROWS, width), F32),
            pltpu.VMEM((6, 16, 128), F32),
            pltpu.VMEM((5, NY - 1, 16, 128), F32),
            pltpu.SemaphoreType.DMA((N_COPIES,)),
            pltpu.SemaphoreType.DMA((N_COPIES,)),
        ],
        compiler_params=pltpu.CompilerParams(
            collective_id=0, has_side_effects=True, vmem_limit_bytes=48 * 1024 * 1024
        ),
        cost_estimate=pl.CostEstimate(flops=3 * 2 * 512 * 512 * D, bytes_accessed=1 << 20, transcendentals=1 << 20),
        name="pair_gradients",
    )(images, texts, log_scale, bias)


def solution(mesh):
    rows = P(("dp", "group"), None)
    return jax.shard_map(
        shards, mesh=mesh, in_specs=(rows, rows, P(), P()), out_specs=(rows, rows, P()), check_vma=False
    )
```

time: 1090 us -> 97.6 us (0.09)
  blocking collectives: 799 us -> 0 us
  waiting for transfers between devices: 146 us -> 0 us
  Pallas kernels: 0 us -> 90.8 us
  starting transfers between devices: 87 us -> 0 us
  between operations: 17.1 us -> 1.94 us
  local copies, waits for them, and re-layouts: 15.7 us -> 3.31 us
    unnamed x2 -> x0, blocking collectives: 606 us -> none
    psum x1 -> x0, blocking collectives: 150 us -> none  [shards(): lax.psum((partial_sums[0], partial_sums[1]), ('dp', 'group'))]
    all_gather x1 -> x0, waiting for transfers between devices: 145 us -> none  [shards(): right = lax.all_gather(txt_b, 'dp', axis=0, tiled=True)]
    pallas_call x0 -> x1, Pallas kernels: none -> 90.8 us  [shards(): pl.pallas_call(kernel, out_shape=(jax.ShapeDtypeStruct((ROWS, D), F32), j...]
    unnamed x20 -> x0, starting transfers between devices: 86.9 us -> none
    all_gather x1 -> x0, blocking collectives: 43.7 us -> none  [shards(): left = lax.all_gather(img_b, 'group', axis=0, tiled=True)]
    unnamed x14 -> x7, local copies, waits for them, and re-layouts: 15.6 us -> 3.31 us
  transfers between devices with their start and end apart: 21 -> 0, of which waited for: 2 -> 0; matrix products, arithmetic and copies ran while one was open for 53% -> 0% of each run, Pallas kernels for 0% -> 0%
where the time goes in v1:
time: 97.6 us; the launch traced here: 96.1 us
  Pallas kernels  90.8 us (93%)
  local copies, waits for them, and re-layouts  3.31 us (3%)
  between operations  1.94 us (2%)
    pallas_call x1, Pallas kernels, shards(): pl.pallas_call(kernel, out_shape=(jax.ShapeDtypeStruct((ROWS, D), F32), j...  90.8 us
    unnamed x7, local copies, waits for them, and re-layouts  3.31 us

profile of v1, /device:TPU:1, one launch (start us, length us, event | category | flops | bytes accessed | tf_op | source)
XLA Modules:
  0.0 96.1 jit_solution(170073601243997362)
XLA Ops:
  1.9 0.0 copy-start
  1.9 0.8 copy-done
  2.7 0.0 copy-start.1
  2.7 0.8 copy-done.1
  3.5 90.8 %pair_gradients.1 = (f32[12,1152]{1,0:T(8,128)S(1)}, f32[12,1152]{1,0:T(8,128)S(1)}, f32[2]{0:T(128)S(1)}) custom-call(bf16[12,1152]{1,0:T(8,128)(2,1)S(1)} %copy-done, bf16[12,1152]{1,0:T(8,128)(2,1)S(1)} %copy-done.1, f32[1]{0:T(128)S(6)} %copy.10.ls_ref, f32[1]{0:T(128)S(6)} %copy.11.bias_ref), custom_call_target="tpu_custom_call" | custom-call | flops 1811939328 | bytes 1048576 | tf_op jit(solution)/shard_map/pair_gradients/pallas_call | solution.py:252
  94.3 0.6 copy.12
  94.9 0.6 copy.13
  95.6 0.5 copy.14
Async XLA Ops:
  1.9 0.8 copy-start
  2.7 0.8 copy-start.1

commit v2 on v1

v2 whole, which is shorter than its diff:
```python
import jax
import jax.numpy as jnp
from jax import lax
from jax.experimental import pallas as pl
from jax.experimental.pallas import tpu as pltpu
from jax.sharding import PartitionSpec as P

D = 1152
ROWS = 12
PAD = 16
X, Y, Z = 4, 8, 16
Y_OFF = (0, 1, -1, 2, -2, 3, -3, 4)
Z_NEAR = (0, 1, -1)
Z_FAR = (0, 8, 4, -4)
Z_LAST = (2, -6, -2, 6)
NX, NY, NN, NF = 4, 8, 4, 4
L_OWN, R_OWN = NN * NF * PAD, NX * NY * PAD
XR, ZR = NY * ROWS, NF * ROWS
WIDTH = 384
NC = D // WIDTH
MESH = pl.DeviceIdType.MESH
F32, BF16 = jnp.float32, jnp.bfloat16
STEP = 64
N_COPIES = 160


def slot(offsets, size, offset):
    return [o % size for o in offsets].index(offset % size)


def window(entry):
    return pl.ds(24 * (entry // 2) + 8 * (entry % 2), PAD)


def kernel(
    img_hbm, txt_hbm, ls_ref, bias_ref, ig_ref, tg_ref, st_ref,
    img_ref, txt_ref, lall, rall, cosb, wt, wb, wtc, wbc, sel, tp, tx1, tx2, ty, ip, iz1, iz2, iw,
    stat, stat_in, load_sem, send_sem, recv_sem,
):
    dp, group = lax.axis_index("dp"), lax.axis_index("group")
    zh, xx, yy = dp % 2, (dp // 2) % X, dp // (2 * X)
    zz, cc = zh * 8 + group // 2, group % 2

    def at(dx=0, dy=0, dz=0, dc=0):
        x, y, z, c = (xx + dx + X) % X, (yy + dy + Y) % Y, (zz + dz + Z) % Z, (cc + dc) % 2
        return ((y * X + x) * 2 + z // 8, (z % 8) * 2 + c)

    loads = [
        pltpu.make_async_copy(img_hbm, img_ref, load_sem.at[0]),
        pltpu.make_async_copy(txt_hbm, txt_ref, load_sem.at[1]),
    ]
    for load in loads:
        load.start()
    partners = [at(dz=d) for d in (8, 4, -4)] + [at(dy=d) for d in Y_OFF[:0:-1]] + [at(dx=d) for d in (2, 1, 3)]
    partners += [at(dz=d) for d in (2, -2, 1, -1)] + [at(dc=1)]
    barrier = pltpu.get_barrier_semaphore()
    for p in partners:
        pl.semaphore_signal(barrier, inc=1, device_id=p, device_id_type=MESH)

    copies = []

    def send(src, dst, device):
        k = len(copies)
        copy = pltpu.make_async_remote_copy(
            src_ref=src, dst_ref=dst, send_sem=send_sem.at[k], recv_sem=recv_sem.at[k],
            device_id=device, device_id_type=MESH,
        )
        copy.start()
        copies.append(copy)
        return copy

    def wait(*got):
        for copy in got:
            copy.wait_recv()

    def unit(ref):
        full = ref[...].astype(F32)
        inverse = lax.rsqrt(jnp.sum(full * full, axis=1, keepdims=True) + 1e-06)
        return full * inverse, inverse

    for load, ref, own in zip(loads, (img_ref, txt_ref), (lall.at[0, 0, 0], rall.at[0, 0, 0])):
        load.wait()
        own[...] = jnp.zeros((PAD, D), BF16)
        own[0:ROWS, :] = unit(ref)[0].astype(BF16)
    r = lax.broadcasted_iota(jnp.int32, sel.shape, 0)
    c = lax.broadcasted_iota(jnp.int32, sel.shape, 1)
    picked = ((c & 15) < ROWS) & ((c >> 4) * ROWS + (c & 15) == r)
    sel[...] = jnp.where(picked, 1.0, 0.0).astype(BF16)
    pl.semaphore_wait(barrier, len(partners))

    img_own, txt_own = lall.at[0, 0], rall.at[0, 0]
    z_got, y_got = {}, {}
    for f in (1, 2, 3):
        to = slot(Z_FAR, Z, -Z_FAR[f])
        z_got[to] = send(img_own.at[0], img_own.at[to], at(dz=Z_FAR[f]))
    for j in (7, 5, 6, 3, 4, 1, 2):
        to = slot(Y_OFF, Y, -Y_OFF[j])
        y_got[to] = send(txt_own.at[0], txt_own.at[to], at(dy=Y_OFF[j]))

    def x_send(lo, hi, straight=False):
        part = pl.ds(lo, hi - lo)
        got = {}
        if straight:
            got[2] = send(txt_own.at[part], rall.at[0, 2, part], at(dx=2))
        got[3] = send(txt_own.at[part], rall.at[0, 3, part], at(dx=1))
        got[1] = send(txt_own.at[part], rall.at[0, 1, part], at(dx=-1))
        return got

    def x_relay(got, frm, lo, hi):
        part = pl.ds(lo, hi - lo)
        wait(got[frm])
        got[2] = send(rall.at[0, frm, part], rall.at[0, 2, part], at(dx=1 if frm == 3 else -1))

    def n_send(lo, hi):
        part = pl.ds(lo, hi - lo)
        return {
            2: send(img_own.at[part], lall.at[0, 2, part], at(dz=1)),
            1: send(img_own.at[part], lall.at[0, 1, part], at(dz=-1)),
        }

    def n_relay(frm, entry):
        offset = Z_NEAR[frm] * 2 + Z_FAR[entry]
        to = slot(Z_LAST, Z, offset)
        return send(lall.at[0, frm, entry], lall.at[0, 3, to], at(dz=-Z_NEAR[frm]))

    n0 = n_send(0, 1)
    x0 = x_send(0, 1)
    wait(y_got[1], y_got[2])
    x1 = x_send(1, 3)
    wait(n0[1], n0[2])
    last = [n_relay(1, 0), n_relay(2, 0)]
    x_relay(x0, 3, 0, 1)
    wait(y_got[3], y_got[4])
    x2 = x_send(3, 5)
    wait(z_got[2], z_got[3])
    n1 = n_send(2, 4)
    x_relay(x1, 1, 1, 3)
    wait(y_got[5], y_got[6], y_got[7])
    x3 = x_send(5, 8, straight=True)
    shared_r = [send(rall.at[0, 0], rall.at[1, 0], at(dc=1))]
    x_relay(x2, 3, 3, 5)
    wait(n1[1], n1[2])
    last += [n_relay(1, 2), n_relay(2, 3)]
    wait(z_got[1])
    n2 = n_send(1, 2)
    shared_l = [send(lall.at[0, 0], lall.at[1, 0], at(dc=1))]
    wait(x0[1], x1[3], x2[1])
    for s in (3, 1, 2):
        wait(x3[s])
        if s == 2:
            wait(x0[2], x1[2], x2[2])
        shared_r.append(send(rall.at[0, s], rall.at[1, s], at(dc=1)))
    for s in (2, 1):
        wait(n2[s])
        shared_l.append(send(lall.at[0, s], lall.at[1, s], at(dc=1)))
    wait(*last)
    shared_l.append(send(lall.at[0, 3], lall.at[1, 3], at(dc=1)))

    scale = jnp.exp(jnp.full((1, 1), ls_ref[0], F32))
    shift = jnp.full((1, 1), bias_ref[0], F32)
    dims = (((1,), (1,)), ((), ()))

    def sigmoid(logit):
        return 1.0 / (1.0 + jnp.exp(-logit))

    def row_blocks(core, ref, n):
        return ref.at[core].reshape(n, D)

    left = [row_blocks(i, lall, L_OWN) for i in range(2)]
    right = [row_blocks(i, rall, R_OWN) for i in range(2)]
    row_ok = (lax.broadcasted_iota(jnp.int32, (STEP, L_OWN), 0) & 15) < ROWS
    col_ok = (lax.broadcasted_iota(jnp.int32, (STEP, L_OWN), 1) & 15) < ROWS
    ok = jnp.where(row_ok & col_ok, 1.0, 0.0).astype(F32)

    def fold(a):
        return jnp.sum(a.reshape(STEP // 8, 8, a.shape[1]), axis=0)

    def text_weights(core, sums):
        cosb[:, 0:L_OWN] = lax.dot_general(right[0][...], left[core][...], dims, preferred_element_type=F32)
        cols = slice(core * L_OWN, (core + 1) * L_OWN)

        def weigh(i, sums):
            part = pl.ds(pl.multiple_of(i * STEP, STEP), STEP)
            cosine = cosb[part, 0:L_OWN]
            weight = sigmoid(scale * cosine + shift)
            wt[part, cols] = weight.astype(BF16)
            return sums[0] + fold(weight * cosine), sums[1] + fold(weight * ok)

        return lax.fori_loop(0, R_OWN // STEP, weigh, sums)

    def image_weights(core):
        cosb[0:L_OWN, :] = lax.dot_general(left[0][...], right[core][...], dims, preferred_element_type=F32)
        cols = slice(core * R_OWN, (core + 1) * R_OWN)

        def weigh(i, carry):
            part = pl.ds(pl.multiple_of(i * STEP, STEP), STEP)
            wb[part, cols] = sigmoid(scale * cosb[part, :] + shift).astype(BF16)
            return carry

        lax.fori_loop(0, L_OWN // STEP, weigh, 0)

    def lanes(a):
        return sum(a[:, 128 * i : 128 * (i + 1)] for i in range(a.shape[1] // 128))

    rows16 = lax.broadcasted_iota(jnp.int32, (PAD, 128), 0)
    cols16 = lax.broadcasted_iota(jnp.int32, (PAD, 128), 1)
    diagonal = rows16 == cols16
    counted = jnp.where(diagonal & (rows16 < ROWS), 1.0, 0.0).astype(F32)

    zero = jnp.zeros((8, L_OWN), F32)
    sums = text_weights(0, (zero, zero))
    cosine = cosb[0:PAD, 0:128]
    logit = scale * cosine + shift
    other, same = sigmoid(logit), -sigmoid(-logit)
    wt[0:PAD, 0:128] = jnp.where(diagonal, same, other).astype(BF16)
    change = (same - other) * counted
    change_scale = change * cosine
    wait(*shared_l)
    sums = text_weights(1, sums)
    stat[0, 0:8, :] = (lanes(sums[0]) + change_scale[0:8] + change_scale[8:16]) * scale
    stat[0, 8:16, :] = lanes(sums[1]) + change[0:8] + change[8:16]

    def stat_send(level, devices):
        return [send(stat.at[level], stat_in.at[level, i], d) for i, d in enumerate(devices)]

    def stat_take(level, got):
        wait(*got)
        total = stat[level]
        for i in range(len(got)):
            total += stat_in[level, i]
        stat[level + 1] = total

    stat_got = stat_send(0, [at(dz=d) for d in Z_FAR[1:]])
    wtc[...] = jnp.dot(sel[...], wt[...], preferred_element_type=F32).astype(BF16)

    def cols_of(k):
        return pl.ds(k * WIDTH, WIDTH)

    x_in, z_in = {}, {}

    def text_part(k):
        t = jnp.dot(wtc[:, 0:L_OWN], left[0][:, cols_of(k)], preferred_element_type=F32)
        t += jnp.dot(wtc[:, L_OWN : 2 * L_OWN], left[1][:, cols_of(k)], preferred_element_type=F32)
        tp[k] = t.reshape(NX, XR, WIDTH)
        x_in[k] = [
            send(tp.at[k, 2, pl.ds(0, XR // 2)], tx1.at[k, 0], at(dx=1)),
            send(tp.at[k, 2, pl.ds(XR // 2, XR // 2)], tx1.at[k, 1], at(dx=-1)),
        ]

    def image_part(k):
        m = jnp.dot(wbc[:, 0:R_OWN], right[0][:, cols_of(k)], preferred_element_type=F32)
        m += jnp.dot(wbc[:, R_OWN : 2 * R_OWN], right[1][:, cols_of(k)], preferred_element_type=F32)
        ip[k] = m.reshape(NN, ZR, WIDTH)
        z_in[k] = [
            send(ip.at[k, 3, pl.ds(0, ZR // 2)], iz1.at[k, 0], at(dz=1)),
            send(ip.at[k, 3, pl.ds(ZR // 2, ZR // 2)], iz1.at[k, 1], at(dz=-1)),
        ]

    text_part(0)
    image_weights(0)
    logit = scale * cosb[0:PAD, 0:128] + shift
    wb[0:PAD, 0:128] = jnp.where(diagonal, -sigmoid(-logit), sigmoid(logit)).astype(BF16)
    wait(*shared_r)
    image_weights(1)
    wbc[...] = jnp.dot(sel[0 : NN * ZR, 0:L_OWN], wb[...], preferred_element_type=F32).astype(BF16)
    image_part(0)
    for k in range(1, NC):
        text_part(k)
        image_part(k)

    f_in, y_in = {}, {}
    for k in range(NC):
        wait(*x_in[k])
        tp[k, 1, 0 : XR // 2] += tx1[k, 0]
        tp[k, 3, XR // 2 : XR] += tx1[k, 1]
        x_in[k] = [send(tp.at[k, 1], tx2.at[k, 0], at(dx=1)), send(tp.at[k, 3], tx2.at[k, 1], at(dx=-1))]
        wait(*z_in[k])
        ip[k, 1, 0 : ZR // 2] += iz1[k, 0]
        ip[k, 2, 0 : ZR // 2] += iz1[k, 1]
        z_in[k] = [send(ip.at[k, 1], iz2.at[k, 0], at(dz=1)), send(ip.at[k, 2], iz2.at[k, 1], at(dz=-1))]
    stat_take(0, stat_got)
    stat_got = stat_send(1, [at(dy=d) for d in Y_OFF[1:]])
    for k in range(NC):
        wait(*z_in[k])
        ip[k, 0] += iz2[k, 0] + iz2[k, 1]
        f_in[k] = [send(ip.at[k, 0, window(f)], iw.at[k, f - 1], at(dz=Z_FAR[f])) for f in (1, 2, 3)]
        wait(*x_in[k])
        tp[k, 0] += tx2[k, 0] + tx2[k, 1]
        y_in[k] = [send(tp.at[k, 0, window(j)], ty.at[k, j - 1], at(dy=Y_OFF[j])) for j in (7, 5, 6, 3, 4, 1, 2)]
        if k == 0:
            stat_take(1, stat_got)
            stat_got = stat_send(2, [at(dx=d) for d in (1, 2, 3)])
    stat_take(2, stat_got)
    stat_got = stat_send(3, [at(dz=d) for d in (2, 1, -1)])

    def total_of(own, ref, k, n):
        even, odd = own, None
        for e in range(1, n):
            got = ref[k, e - 1]
            if e % 2 == 0:
                even = even + got
            else:
                odd = got if odd is None else odd + got
        return even[0:ROWS] + odd[PAD - ROWS : PAD]

    def back(ref, total, out_ref):
        u, inverse = unit(ref)
        grad = scale * total
        out_ref[...] = (grad - u * jnp.sum(u * grad, axis=1, keepdims=True)) * inverse

    for k in range(NC):
        wait(*f_in[k])
    back(img_ref, jnp.concatenate([total_of(ip[k, 0, 0:PAD], iw, k, NF) for k in range(NC)], axis=1), ig_ref)
    stat_take(3, stat_got)
    stat_got = stat_send(4, [at(dc=1)])
    for k in range(NC):
        wait(*y_in[k])
    back(txt_ref, jnp.concatenate([total_of(tp[k, 0, 0:PAD], ty, k, NY) for k in range(NC)], axis=1), tg_ref)
    stat_take(4, stat_got)
    st_ref[0] = jnp.sum(stat[5, 0:8, :])
    st_ref[1] = jnp.sum(stat[5, 8:16, :])
    for copy in copies:
        copy.wait_send()


def shards(images, texts, log_scale, bias):
    vmem, smem = pl.BlockSpec(memory_space=pltpu.VMEM), pl.BlockSpec(memory_space=pltpu.SMEM)
    hbm = pl.BlockSpec(memory_space=pltpu.HBM)
    return pl.pallas_call(
        kernel,
        out_shape=(
            jax.ShapeDtypeStruct((ROWS, D), F32),
            jax.ShapeDtypeStruct((ROWS, D), F32),
            jax.ShapeDtypeStruct((2,), F32),
        ),
        in_specs=[hbm, hbm, smem, smem],
        out_specs=(vmem, vmem, smem),
        scratch_shapes=[
            pltpu.VMEM((ROWS, D), BF16),
            pltpu.VMEM((ROWS, D), BF16),
            pltpu.VMEM((2, NN, NF, PAD, D), BF16),
            pltpu.VMEM((2, NX, NY, PAD, D), BF16),
            pltpu.VMEM((R_OWN, R_OWN), F32),
            pltpu.VMEM((R_OWN, 2 * L_OWN), BF16),
            pltpu.VMEM((L_OWN, 2 * R_OWN), BF16),
            pltpu.VMEM((NX * XR, 2 * L_OWN), BF16),
            pltpu.VMEM((NN * ZR, 2 * R_OWN), BF16),
            pltpu.VMEM((NX * XR, R_OWN), BF16),
            pltpu.VMEM((NC, NX, XR, WIDTH), F32),
            pltpu.VMEM((NC, 2, XR // 2, WIDTH), F32),
            pltpu.VMEM((NC, 2, XR, WIDTH), F32),
            pltpu.VMEM((NC, NY - 1, PAD, WIDTH), F32),
            pltpu.VMEM((NC, NN, ZR, WIDTH), F32),
            pltpu.VMEM((NC, 2, ZR // 2, WIDTH), F32),
            pltpu.VMEM((NC, 2, ZR, WIDTH), F32),
            pltpu.VMEM((NC, NF - 1, PAD, WIDTH), F32),
            pltpu.VMEM((6, 16, 128), F32),
            pltpu.VMEM((5, NY - 1, 16, 128), F32),
            pltpu.SemaphoreType.DMA((2,)),
            pltpu.SemaphoreType.DMA((N_COPIES,)),
            pltpu.SemaphoreType.DMA((N_COPIES,)),
        ],
        compiler_params=pltpu.CompilerParams(
            collective_id=0, has_side_effects=True, vmem_limit_bytes=48 * 1024 * 1024
        ),
        cost_estimate=pl.CostEstimate(flops=3 * 2 * 512 * 512 * D, bytes_accessed=1 << 20, transcendentals=1 << 20),
        name="pair_gradients",
    )(images, texts, log_scale, bias)


def solution(mesh):
    rows = P(("dp", "group"), None)
    return jax.shard_map(
        shards, mesh=mesh, in_specs=(rows, rows, P(), P()), out_specs=(rows, rows, P()), check_vma=False
    )
```

time: 97.6 us -> 89.1 us (0.913); the launches traced: 96.1 us -> 88.8 us
  Pallas kernels: 90.8 us -> 83.6 us
    pallas_call x1, Pallas kernels: 90.8 us -> 83.6 us  [shards(): pl.pallas_call(kernel, out_shape=(jax.ShapeDtypeStruct((ROWS, D), F32), j...]
where the time goes in v2:
time: 89.1 us; the launch traced here: 88.8 us
  Pallas kernels  83.6 us (94%)
  local copies, waits for them, and re-layouts  3.31 us (4%)
  between operations  1.94 us (2%)
    pallas_call x1, Pallas kernels, shards(): pl.pallas_call(kernel, out_shape=(jax.ShapeDtypeStruct((ROWS, D), F32), j...  83.6 us
    unnamed x7, local copies, waits for them, and re-layouts  3.31 us

profile of v2, /device:TPU:1, one launch (start us, length us, event | category | flops | bytes accessed | tf_op | source)
XLA Modules:
  0.0 88.8 jit_solution(14506123770233726083)
XLA Ops:
  1.9 0.0 copy-start
  1.9 0.8 copy-done
  2.7 0.0 copy-start.1
  2.7 0.8 copy-done.1
  3.5 83.6 %pair_gradients.1 = (f32[12,1152]{1,0:T(8,128)S(1)}, f32[12,1152]{1,0:T(8,128)S(1)}, f32[2]{0:T(128)S(1)}) custom-call(bf16[12,1152]{1,0:T(8,128)(2,1)S(1)} %copy-done, bf16[12,1152]{1,0:T(8,128)(2,1)S(1)} %copy-done.1, f32[1]{0:T(128)S(6)} %copy.10.ls_ref, f32[1]{0:T(128)S(6)} %copy.11.bias_ref), custom_call_target="tpu_custom_call" | custom-call | flops 1811939328 | bytes 1048576 | tf_op jit(solution)/shard_map/pair_gradients/pallas_call | solution.py:329
  87.0 0.6 copy.12
  87.7 0.6 copy.13
  88.3 0.5 copy.14
Async XLA Ops:
  1.9 0.8 copy-start
  2.7 0.8 copy-start.1

commit v3 on v2

--- a/solution.py
+++ b/solution.py
@@ -18,6 +18,7 @@
 XR, ZR = NY * ROWS, NF * ROWS
 WIDTH = 384
 NC = D // WIDTH
+SPLIT = 896
 MESH = pl.DeviceIdType.MESH
 F32, BF16 = jnp.float32, jnp.bfloat16
 STEP = 64
@@ -57,17 +58,30 @@
     for p in partners:
         pl.semaphore_signal(barrier, inc=1, device_id=p, device_id_type=MESH)
 
-    copies = []
-
-    def send(src, dst, device):
-        k = len(copies)
-        copy = pltpu.make_async_remote_copy(
+    taken, unsent = [0], []
+
+    def remote(k, src, dst, device):
+        return pltpu.make_async_remote_copy(
             src_ref=src, dst_ref=dst, send_sem=send_sem.at[k], recv_sem=recv_sem.at[k],
             device_id=device, device_id_type=MESH,
         )
-        copy.start()
-        copies.append(copy)
+
+    def send_all(parts, whole):
+        k = taken[0]
+        taken[0] += 1
+        for src, dst, device in parts:
+            remote(k, src, dst, device).start()
+        copy = remote(k, whole, whole, parts[0][2])
+        unsent.append(copy)
         return copy
+
+    def send(src, dst, device):
+        return send_all([(src, dst, device)], dst)
+
+    def wait_sent(n):
+        for copy in unsent[:n]:
+            copy.wait_send()
+        del unsent[:n]
 
     def wait(*got):
         for copy in got:
@@ -89,27 +103,41 @@
     pl.semaphore_wait(barrier, len(partners))
 
     img_own, txt_own = lall.at[0, 0], rall.at[0, 0]
-    z_got, y_got = {}, {}
-    for f in (1, 2, 3):
-        to = slot(Z_FAR, Z, -Z_FAR[f])
-        z_got[to] = send(img_own.at[0], img_own.at[to], at(dz=Z_FAR[f]))
-    for j in (7, 5, 6, 3, 4, 1, 2):
-        to = slot(Y_OFF, Y, -Y_OFF[j])
-        y_got[to] = send(txt_own.at[0], txt_own.at[to], at(dy=Y_OFF[j]))
+    def far_first(lo, hi):
+        to = [slot(Z_FAR, Z, -Z_FAR[f]) for f in range(lo, hi)]
+        parts = [(img_own.at[0], img_own.at[t], at(dz=Z_FAR[f])) for t, f in zip(to, range(lo, hi))]
+        return send_all(parts, img_own.at[pl.ds(lo, hi - lo)])
+
+    main, rest = pl.ds(0, SPLIT), pl.ds(SPLIT, D - SPLIT)
+
+    def y_first(*entries):
+        to = [slot(Y_OFF, Y, -Y_OFF[j]) for j in entries]
+        parts = [(txt_own.at[0, :, main], txt_own.at[t, :, main], at(dy=Y_OFF[j])) for t, j in zip(to, entries)]
+        return send_all(parts, txt_own.at[pl.ds(min(entries), len(entries)), :, main])
+
+    z_eight = far_first(1, 2)
+    x_rest = send_all(
+        [(rall.at[0, 0, 0, :, rest], rall.at[0, X - d, 0, :, rest], at(dx=d)) for d in (2, 1, 3)],
+        rall.at[0, pl.ds(1, NX - 1), 0, :, rest],
+    )
+    y_far = y_first(7, 5, 6)
+    z_four = far_first(2, 4)
+    y_two, y_one = y_first(3, 4), y_first(1, 2)
 
     def x_send(lo, hi, straight=False):
         part = pl.ds(lo, hi - lo)
         got = {}
         if straight:
-            got[2] = send(txt_own.at[part], rall.at[0, 2, part], at(dx=2))
-        got[3] = send(txt_own.at[part], rall.at[0, 3, part], at(dx=1))
-        got[1] = send(txt_own.at[part], rall.at[0, 1, part], at(dx=-1))
+            got[2] = send(txt_own.at[part, :, main], rall.at[0, 2, part, :, main], at(dx=2))
+        got[3] = send(txt_own.at[part, :, main], rall.at[0, 3, part, :, main], at(dx=1))
+        got[1] = send(txt_own.at[part, :, main], rall.at[0, 1, part, :, main], at(dx=-1))
         return got
 
     def x_relay(got, frm, lo, hi):
         part = pl.ds(lo, hi - lo)
         wait(got[frm])
-        got[2] = send(rall.at[0, frm, part], rall.at[0, 2, part], at(dx=1 if frm == 3 else -1))
+        to = at(dx=1 if frm == 3 else -1)
+        got[2] = send(rall.at[0, frm, part, :, main], rall.at[0, 2, part, :, main], to)
 
     def n_send(lo, hi):
         part = pl.ds(lo, hi - lo)
@@ -125,26 +153,33 @@
 
     n0 = n_send(0, 1)
     x0 = x_send(0, 1)
-    wait(y_got[1], y_got[2])
+    wait(x_rest)
+    near = [(j, slot(Y_OFF, Y, -Y_OFF[j])) for j in (7, 5, 6, 3, 4, 1, 2)]
+    y_rest = send_all(
+        [(rall.at[0, :, 0, :, rest], rall.at[0, :, t, :, rest], at(dy=Y_OFF[j])) for j, t in near],
+        rall.at[0, :, pl.ds(1, NY - 1), :, rest],
+    )
+    wait(y_one)
     x1 = x_send(1, 3)
     wait(n0[1], n0[2])
     last = [n_relay(1, 0), n_relay(2, 0)]
     x_relay(x0, 3, 0, 1)
-    wait(y_got[3], y_got[4])
+    wait(y_two)
     x2 = x_send(3, 5)
-    wait(z_got[2], z_got[3])
+    wait(z_four)
     n1 = n_send(2, 4)
     x_relay(x1, 1, 1, 3)
-    wait(y_got[5], y_got[6], y_got[7])
+    wait(y_far)
     x3 = x_send(5, 8, straight=True)
-    shared_r = [send(rall.at[0, 0], rall.at[1, 0], at(dc=1))]
     x_relay(x2, 3, 3, 5)
     wait(n1[1], n1[2])
     last += [n_relay(1, 2), n_relay(2, 3)]
-    wait(z_got[1])
+    wait(z_eight)
     n2 = n_send(1, 2)
     shared_l = [send(lall.at[0, 0], lall.at[1, 0], at(dc=1))]
     wait(x0[1], x1[3], x2[1])
+    wait(y_rest)
+    shared_r = [send(rall.at[0, 0], rall.at[1, 0], at(dc=1))]
     for s in (3, 1, 2):
         wait(x3[s])
         if s == 2:
@@ -221,12 +256,13 @@
     stat[0, 8:16, :] = lanes(sums[1]) + change[0:8] + change[8:16]
 
     def stat_send(level, devices):
-        return [send(stat.at[level], stat_in.at[level, i], d) for i, d in enumerate(devices)]
-
-    def stat_take(level, got):
-        wait(*got)
+        parts = [(stat.at[level], stat_in.at[level, i], d) for i, d in enumerate(devices)]
+        return send_all(parts, stat_in.at[level, pl.ds(0, len(parts))])
+
+    def stat_take(level, got, n):
+        wait(got)
         total = stat[level]
-        for i in range(len(got)):
+        for i in range(n):
             total += stat_in[level, i]
         stat[level + 1] = total
 
@@ -256,42 +292,54 @@
             send(ip.at[k, 3, pl.ds(ZR // 2, ZR // 2)], iz1.at[k, 1], at(dz=-1)),
         ]
 
-    text_part(0)
+    old = len(unsent)
+    f_in, y_in = {}, {}
+
+    def text_merge(k):
+        wait(*x_in[k])
+        tp[k, 1, 0 : XR // 2] += tx1[k, 0]
+        tp[k, 3, XR // 2 : XR] += tx1[k, 1]
+        x_in[k] = [send(tp.at[k, 1], tx2.at[k, 0], at(dx=1)), send(tp.at[k, 3], tx2.at[k, 1], at(dx=-1))]
+
+    def image_merge(k):
+        wait(*z_in[k])
+        ip[k, 1, 0 : ZR // 2] += iz1[k, 0]
+        ip[k, 2, 0 : ZR // 2] += iz1[k, 1]
+        z_in[k] = [send(ip.at[k, 1], iz2.at[k, 0], at(dz=1)), send(ip.at[k, 2], iz2.at[k, 1], at(dz=-1))]
+
+    for k in range(NC):
+        text_part(k)
     image_weights(0)
     logit = scale * cosb[0:PAD, 0:128] + shift
     wb[0:PAD, 0:128] = jnp.where(diagonal, -sigmoid(-logit), sigmoid(logit)).astype(BF16)
     wait(*shared_r)
     image_weights(1)
     wbc[...] = jnp.dot(sel[0 : NN * ZR, 0:L_OWN], wb[...], preferred_element_type=F32).astype(BF16)
-    image_part(0)
-    for k in range(1, NC):
-        text_part(k)
+    for k in range(NC):
         image_part(k)
-
-    f_in, y_in = {}, {}
-    for k in range(NC):
-        wait(*x_in[k])
-        tp[k, 1, 0 : XR // 2] += tx1[k, 0]
-        tp[k, 3, XR // 2 : XR] += tx1[k, 1]
-        x_in[k] = [send(tp.at[k, 1], tx2.at[k, 0], at(dx=1)), send(tp.at[k, 3], tx2.at[k, 1], at(dx=-1))]
-        wait(*z_in[k])
-        ip[k, 1, 0 : ZR // 2] += iz1[k, 0]
-        ip[k, 2, 0 : ZR // 2] += iz1[k, 1]
-        z_in[k] = [send(ip.at[k, 1], iz2.at[k, 0], at(dz=1)), send(ip.at[k, 2], iz2.at[k, 1], at(dz=-1))]
-    stat_take(0, stat_got)
+        text_merge(k)
+    wait_sent(old)
+    for k in range(NC):
+        image_merge(k)
+    stat_take(0, stat_got, NF - 1)
+    old = len(unsent)
     stat_got = stat_send(1, [at(dy=d) for d in Y_OFF[1:]])
     for k in range(NC):
         wait(*z_in[k])
         ip[k, 0] += iz2[k, 0] + iz2[k, 1]
-        f_in[k] = [send(ip.at[k, 0, window(f)], iw.at[k, f - 1], at(dz=Z_FAR[f])) for f in (1, 2, 3)]
+        f_in[k] = send_all([(ip.at[k, 0, window(f)], iw.at[k, f - 1], at(dz=Z_FAR[f])) for f in (1, 2, 3)], iw.at[k])
         wait(*x_in[k])
         tp[k, 0] += tx2[k, 0] + tx2[k, 1]
-        y_in[k] = [send(tp.at[k, 0, window(j)], ty.at[k, j - 1], at(dy=Y_OFF[j])) for j in (7, 5, 6, 3, 4, 1, 2)]
+        y_in[k] = send_all(
+            [(tp.at[k, 0, window(j)], ty.at[k, j - 1], at(dy=Y_OFF[j])) for j in (7, 5, 6, 3, 4, 1, 2)], ty.at[k]
+        )
         if k == 0:
-            stat_take(1, stat_got)
+            stat_take(1, stat_got, NY - 1)
             stat_got = stat_send(2, [at(dx=d) for d in (1, 2, 3)])
-    stat_take(2, stat_got)
+    stat_take(2, stat_got, NX - 1)
     stat_got = stat_send(3, [at(dz=d) for d in (2, 1, -1)])
+
+    wait_sent(old)
 
     def total_of(own, ref, k, n):
         even, odd = own, None
@@ -309,18 +357,17 @@
         out_ref[...] = (grad - u * jnp.sum(u * grad, axis=1, keepdims=True)) * inverse
 
     for k in range(NC):
-        wait(*f_in[k])
+        wait(f_in[k])
     back(img_ref, jnp.concatenate([total_of(ip[k, 0, 0:PAD], iw, k, NF) for k in range(NC)], axis=1), ig_ref)
-    stat_take(3, stat_got)
+    stat_take(3, stat_got, 3)
     stat_got = stat_send(4, [at(dc=1)])
     for k in range(NC):
-        wait(*y_in[k])
+        wait(y_in[k])
     back(txt_ref, jnp.concatenate([total_of(tp[k, 0, 0:PAD], ty, k, NY) for k in range(NC)], axis=1), tg_ref)
-    stat_take(4, stat_got)
+    stat_take(4, stat_got, 1)
     st_ref[0] = jnp.sum(stat[5, 0:8, :])
     st_ref[1] = jnp.sum(stat[5, 8:16, :])
-    for copy in copies:
-        copy.wait_send()
+    wait_sent(len(unsent))
 
 
 def shards(images, texts, log_scale, bias):

time: 89.1 us -> 88.5 us (level)
  Pallas kernels: 83.6 us -> 82.2 us
    pallas_call x1, Pallas kernels: 83.6 us -> 82.2 us  [shards(): pl.pallas_call(kernel, out_shape=(jax.ShapeDtypeStruct((ROWS, D), F32), j...]
where the time goes in v3:
time: 88.5 us; the launch traced here: 87.4 us
  Pallas kernels  82.2 us (93%)
  local copies, waits for them, and re-layouts  3.31 us (4%)
  between operations  1.94 us (2%)
    pallas_call x1, Pallas kernels, shards(): pl.pallas_call(kernel, out_shape=(jax.ShapeDtypeStruct((ROWS, D), F32), j...  82.2 us
    unnamed x7, local copies, waits for them, and re-layouts  3.31 us

profile of v3, /device:TPU:1, one launch (start us, length us, event | category | flops | bytes accessed | tf_op | source)
XLA Modules:
  0.0 87.4 jit_solution(13091390204981775900)
XLA Ops:
  1.9 0.0 copy-start
  1.9 0.8 copy-done
  2.7 0.0 copy-start.1
  2.7 0.8 copy-done.1
  3.5 82.2 %pair_gradients.1 = (f32[12,1152]{1,0:T(8,128)S(1)}, f32[12,1152]{1,0:T(8,128)S(1)}, f32[2]{0:T(128)S(1)}) custom-call(bf16[12,1152]{1,0:T(8,128)(2,1)S(1)} %copy-done, bf16[12,1152]{1,0:T(8,128)(2,1)S(1)} %copy-done.1, f32[1]{0:T(128)S(6)} %copy.10.ls_ref, f32[1]{0:T(128)S(6)} %copy.11.bias_ref), custom_call_target="tpu_custom_call" | custom-call | flops 1811939328 | bytes 1048576 | tf_op jit(solution)/shard_map/pair_gradients/pallas_call | solution.py:376
  85.7 0.6 copy.12
  86.3 0.6 copy.13
  86.9 0.5 copy.14
Async XLA Ops:
  1.9 0.8 copy-start
  2.7 0.8 copy-start.1

commit v4 on v3

--- a/solution.py
+++ b/solution.py
@@ -35,7 +35,7 @@
 
 def kernel(
     img_hbm, txt_hbm, ls_ref, bias_ref, ig_ref, tg_ref, st_ref,
-    img_ref, txt_ref, lall, rall, cosb, wt, wb, wtc, wbc, sel, tp, tx1, tx2, ty, ip, iz1, iz2, iw,
+    img_ref, txt_ref, lall, rall, cosb, wt, wb, wtc, wbc, sel, tp, tx1, tx2, ty, ip, iz1, iz2, iw, fb,
     stat, stat_in, load_sem, send_sem, recv_sem,
 ):
     dp, group = lax.axis_index("dp"), lax.axis_index("group")
@@ -52,7 +52,7 @@
     ]
     for load in loads:
         load.start()
-    partners = [at(dz=d) for d in (8, 4, -4)] + [at(dy=d) for d in Y_OFF[:0:-1]] + [at(dx=d) for d in (2, 1, 3)]
+    partners = [at(dz=d) for d in (4, -4)] + [at(dy=d) for d in Y_OFF[:0:-1]] + [at(dx=d) for d in (2, 1, 3)]
     partners += [at(dz=d) for d in (2, -2, 1, -1)] + [at(dc=1)]
     barrier = pltpu.get_barrier_semaphore()
     for p in partners:
@@ -103,11 +103,6 @@
     pl.semaphore_wait(barrier, len(partners))
 
     img_own, txt_own = lall.at[0, 0], rall.at[0, 0]
-    def far_first(lo, hi):
-        to = [slot(Z_FAR, Z, -Z_FAR[f]) for f in range(lo, hi)]
-        parts = [(img_own.at[0], img_own.at[t], at(dz=Z_FAR[f])) for t, f in zip(to, range(lo, hi))]
-        return send_all(parts, img_own.at[pl.ds(lo, hi - lo)])
-
     main, rest = pl.ds(0, SPLIT), pl.ds(SPLIT, D - SPLIT)
 
     def y_first(*entries):
@@ -115,13 +110,13 @@
         parts = [(txt_own.at[0, :, main], txt_own.at[t, :, main], at(dy=Y_OFF[j])) for t, j in zip(to, entries)]
         return send_all(parts, txt_own.at[pl.ds(min(entries), len(entries)), :, main])
 
-    z_eight = far_first(1, 2)
+    z_below = send(img_own.at[0], img_own.at[3], at(dz=4))
+    z_above = send(img_own.at[0], img_own.at[2], at(dz=-4))
     x_rest = send_all(
         [(rall.at[0, 0, 0, :, rest], rall.at[0, X - d, 0, :, rest], at(dx=d)) for d in (2, 1, 3)],
         rall.at[0, pl.ds(1, NX - 1), 0, :, rest],
     )
     y_far = y_first(7, 5, 6)
-    z_four = far_first(2, 4)
     y_two, y_one = y_first(3, 4), y_first(1, 2)
 
     def x_send(lo, hi, straight=False):
@@ -161,16 +156,24 @@
     )
     wait(y_one)
     x1 = x_send(1, 3)
-    wait(n0[1], n0[2])
-    last = [n_relay(1, 0), n_relay(2, 0)]
     x_relay(x0, 3, 0, 1)
     wait(y_two)
     x2 = x_send(3, 5)
-    wait(z_four)
+    wait(z_below, z_above)
+    low, high = pl.ds(0, 640), pl.ds(640, D - 640)
+    z_eight = send_all(
+        [
+            (img_own.at[3, :, low], img_own.at[1, :, low], at(dz=4)),
+            (img_own.at[2, :, high], img_own.at[1, :, high], at(dz=-4)),
+        ],
+        img_own.at[1],
+    )
     n1 = n_send(2, 4)
-    x_relay(x1, 1, 1, 3)
+    wait(n0[1], n0[2])
+    last = [n_relay(1, 0), n_relay(2, 0)]
     wait(y_far)
     x3 = x_send(5, 8, straight=True)
+    x_relay(x1, 1, 1, 3)
     x_relay(x2, 3, 3, 5)
     wait(n1[1], n1[2])
     last += [n_relay(1, 2), n_relay(2, 3)]
@@ -266,7 +269,7 @@
             total += stat_in[level, i]
         stat[level + 1] = total
 
-    stat_got = stat_send(0, [at(dz=d) for d in Z_FAR[1:]])
+    stat_got = stat_send(0, [at(dz=4), at(dz=-4)])
     wtc[...] = jnp.dot(sel[...], wt[...], preferred_element_type=F32).astype(BF16)
 
     def cols_of(k):
@@ -318,32 +321,48 @@
     for k in range(NC):
         image_part(k)
         text_merge(k)
+        if k == 0:
+            stat_take(0, stat_got, 2)
+            stat_got = send(stat_in.at[0, 0], stat_in.at[1, 0], at(dz=4))
     wait_sent(old)
     for k in range(NC):
         image_merge(k)
-    stat_take(0, stat_got, NF - 1)
     old = len(unsent)
-    stat_got = stat_send(1, [at(dy=d) for d in Y_OFF[1:]])
-    for k in range(NC):
+    def far_send(k, entry):
+        return send(ip.at[k, 0, window(entry)], iw.at[k, entry - 1], at(dz=Z_FAR[entry]))
+
+    for k in range(NC):
+        over, other = (2, 3) if k % 2 == 0 else (3, 2)
         wait(*z_in[k])
         ip[k, 0] += iz2[k, 0] + iz2[k, 1]
-        f_in[k] = send_all([(ip.at[k, 0, window(f)], iw.at[k, f - 1], at(dz=Z_FAR[f])) for f in (1, 2, 3)], iw.at[k])
+        f_in[k] = [
+            send(ip.at[k, 0, window(1)], iw.at[k, 0], at(dz=Z_FAR[over])),
+            far_send(k, other),
+        ]
         wait(*x_in[k])
         tp[k, 0] += tx2[k, 0] + tx2[k, 1]
         y_in[k] = send_all(
             [(tp.at[k, 0, window(j)], ty.at[k, j - 1], at(dy=Y_OFF[j])) for j in (7, 5, 6, 3, 4, 1, 2)], ty.at[k]
         )
         if k == 0:
-            stat_take(1, stat_got, NY - 1)
-            stat_got = stat_send(2, [at(dx=d) for d in (1, 2, 3)])
-    stat_take(2, stat_got, NX - 1)
-    stat_got = stat_send(3, [at(dz=d) for d in (2, 1, -1)])
+            stat_take(1, stat_got, 1)
+            stat_got = stat_send(2, [at(dy=d) for d in Y_OFF[1:]])
+    for k in range(NC):
+        over = 2 if k % 2 == 0 else 3
+        wait(f_in[k][0])
+        if over % 2 == 0:
+            fb[k, 0:ROWS] = ip[k, 0, 24:36] + iw[k, 0, PAD - ROWS : PAD]
+        else:
+            fb[k] = ip[k, 0, 32:48] + iw[k, 0]
+        f_in[k][0] = send(fb.at[k], iw.at[k, over - 1], at(dz=Z_FAR[over]))
+    stat_take(2, stat_got, NY - 1)
+    stat_got = stat_send(3, [at(dx=d) for d in (1, 2, 3)])
 
     wait_sent(old)
 
-    def total_of(own, ref, k, n):
+    def total_of(own, ref, k, entries):
         even, odd = own, None
-        for e in range(1, n):
+        for e in entries:
             got = ref[k, e - 1]
             if e % 2 == 0:
                 even = even + got
@@ -357,16 +376,20 @@
         out_ref[...] = (grad - u * jnp.sum(u * grad, axis=1, keepdims=True)) * inverse
 
     for k in range(NC):
-        wait(f_in[k])
-    back(img_ref, jnp.concatenate([total_of(ip[k, 0, 0:PAD], iw, k, NF) for k in range(NC)], axis=1), ig_ref)
-    stat_take(3, stat_got, 3)
-    stat_got = stat_send(4, [at(dc=1)])
+        wait(*f_in[k])
+    image_sums = [total_of(ip[k, 0, 0:PAD], iw, k, (2, 3)) for k in range(NC)]
+    stat_take(3, stat_got, NX - 1)
+    stat_got = stat_send(4, [at(dz=d) for d in (2, 1, -1)])
+    back(img_ref, jnp.concatenate(image_sums, axis=1), ig_ref)
     for k in range(NC):
         wait(y_in[k])
-    back(txt_ref, jnp.concatenate([total_of(tp[k, 0, 0:PAD], ty, k, NY) for k in range(NC)], axis=1), tg_ref)
-    stat_take(4, stat_got, 1)
-    st_ref[0] = jnp.sum(stat[5, 0:8, :])
-    st_ref[1] = jnp.sum(stat[5, 8:16, :])
+    stat_take(4, stat_got, 3)
+    stat_got = stat_send(5, [at(dc=1)])
+    text_sums = [total_of(tp[k, 0, 0:PAD], ty, k, range(1, NY)) for k in range(NC)]
+    back(txt_ref, jnp.concatenate(text_sums, axis=1), tg_ref)
+    stat_take(5, stat_got, 1)
+    st_ref[0] = jnp.sum(stat[6, 0:8, :])
+    st_ref[1] = jnp.sum(stat[6, 8:16, :])
     wait_sent(len(unsent))
 
 
@@ -401,8 +424,9 @@
             pltpu.VMEM((NC, 2, ZR // 2, WIDTH), F32),
             pltpu.VMEM((NC, 2, ZR, WIDTH), F32),
             pltpu.VMEM((NC, NF - 1, PAD, WIDTH), F32),
-            pltpu.VMEM((6, 16, 128), F32),
-            pltpu.VMEM((5, NY - 1, 16, 128), F32),
+            pltpu.VMEM((NC, PAD, WIDTH), F32),
+            pltpu.VMEM((7, 16, 128), F32),
+            pltpu.VMEM((6, NY - 1, 16, 128), F32),
             pltpu.SemaphoreType.DMA((2,)),
             pltpu.SemaphoreType.DMA((N_COPIES,)),
             pltpu.SemaphoreType.DMA((N_COPIES,)),

time: 88.5 us -> 87.6 us (0.990)
  no operation moved by 1% of the time
where the time goes in v4:
time: 87.6 us; the launch traced here: 87.3 us
  Pallas kernels  82.1 us (94%)
  local copies, waits for them, and re-layouts  3.31 us (4%)
  between operations  1.94 us (2%)
    pallas_call x1, Pallas kernels, shards(): pl.pallas_call(kernel, out_shape=(jax.ShapeDtypeStruct((ROWS, D), F32), j...  82.1 us
    unnamed x7, local copies, waits for them, and re-layouts  3.31 us

profile of v4, /device:TPU:1, one launch (start us, length us, event | category | flops | bytes accessed | tf_op | source)
XLA Modules:
  0.0 87.3 jit_solution(9597301895276157712)
XLA Ops:
  1.9 0.0 copy-start
  1.9 0.8 copy-done
  2.7 0.0 copy-start.1
  2.7 0.8 copy-done.1
  3.5 82.1 %pair_gradients.1 = (f32[12,1152]{1,0:T(8,128)S(1)}, f32[12,1152]{1,0:T(8,128)S(1)}, f32[2]{0:T(128)S(1)}) custom-call(bf16[12,1152]{1,0:T(8,128)(2,1)S(1)} %copy-done, bf16[12,1152]{1,0:T(8,128)(2,1)S(1)} %copy-done.1, f32[1]{0:T(128)S(6)} %copy.10.ls_ref, f32[1]{0:T(128)S(6)} %copy.11.bias_ref), custom_call_target="tpu_custom_call" | custom-call | flops 1811939328 | bytes 1048576 | tf_op jit(solution)/shard_map/pair_gradients/pallas_call | solution.py:399
  85.6 0.6 copy.12
  86.2 0.6 copy.13
  86.8 0.5 copy.14
Async XLA Ops:
  1.9 0.8 copy-start
  2.7 0.8 copy-start.1

commit v5 on v4

--- a/solution.py
+++ b/solution.py
@@ -16,8 +16,9 @@
 NX, NY, NN, NF = 4, 8, 4, 4
 L_OWN, R_OWN = NN * NF * PAD, NX * NY * PAD
 XR, ZR = NY * ROWS, NF * ROWS
-WIDTH = 384
-NC = D // WIDTH
+WIDTHS = (256, 512, 384)
+BEGINS = (0, 256, 768)
+NC = len(WIDTHS)
 SPLIT = 896
 MESH = pl.DeviceIdType.MESH
 F32, BF16 = jnp.float32, jnp.bfloat16
@@ -29,13 +30,32 @@
     return [o % size for o in offsets].index(offset % size)
 
 
-def window(entry):
-    return pl.ds(24 * (entry // 2) + 8 * (entry % 2), PAD)
+def halves(width):
+    first = 128 * ((width // 128 + 1) // 2)
+    return first, width - first
+
+
+def pack(dst, src, row):
+    width = src.shape[1]
+    first, second = halves(width)
+    dst[:, 0:width] = src[row : row + 8, :]
+    dst[0:4, width : width + first] = src[row + 8 : row + 12, 0:first]
+    dst[4:8, width : width + second] = src[row + 8 : row + 12, first:width]
+    if second < first:
+        dst[4:8, width + second : width + first] = jnp.zeros((4, first - second), F32)
+
+
+def unpack(dst, begin, got):
+    width = [w for w, b in zip(WIDTHS, BEGINS) if b == begin][0]
+    first, second = halves(width)
+    dst[0:8, begin : begin + width] = got[:, 0:width]
+    dst[8:12, begin : begin + first] = got[0:4, width : width + first]
+    dst[8:12, begin + first : begin + width] = got[4:8, width : width + second]
 
 
 def kernel(
     img_hbm, txt_hbm, ls_ref, bias_ref, ig_ref, tg_ref, st_ref,
-    img_ref, txt_ref, lall, rall, cosb, wt, wb, wtc, wbc, sel, tp, tx1, tx2, ty, ip, iz1, iz2, iw, fb,
+    img_ref, txt_ref, lall, rall, cosb, wt, wb, wtc, wbc, sel, tp, tx1, tx2, ty, yb, ip, iz1, iz2, iw, zb, total,
     stat, stat_in, load_sem, send_sem, recv_sem,
 ):
     dp, group = lax.axis_index("dp"), lax.axis_index("group")
@@ -273,26 +293,26 @@
     wtc[...] = jnp.dot(sel[...], wt[...], preferred_element_type=F32).astype(BF16)
 
     def cols_of(k):
-        return pl.ds(k * WIDTH, WIDTH)
+        return pl.ds(BEGINS[k], WIDTHS[k])
 
     x_in, z_in = {}, {}
 
     def text_part(k):
         t = jnp.dot(wtc[:, 0:L_OWN], left[0][:, cols_of(k)], preferred_element_type=F32)
         t += jnp.dot(wtc[:, L_OWN : 2 * L_OWN], left[1][:, cols_of(k)], preferred_element_type=F32)
-        tp[k] = t.reshape(NX, XR, WIDTH)
+        tp[k][...] = t.reshape(NX, XR, WIDTHS[k])
         x_in[k] = [
-            send(tp.at[k, 2, pl.ds(0, XR // 2)], tx1.at[k, 0], at(dx=1)),
-            send(tp.at[k, 2, pl.ds(XR // 2, XR // 2)], tx1.at[k, 1], at(dx=-1)),
+            send(tp[k].at[2, pl.ds(0, XR // 2)], tx1[k].at[0], at(dx=1)),
+            send(tp[k].at[2, pl.ds(XR // 2, XR // 2)], tx1[k].at[1], at(dx=-1)),
         ]
 
     def image_part(k):
         m = jnp.dot(wbc[:, 0:R_OWN], right[0][:, cols_of(k)], preferred_element_type=F32)
         m += jnp.dot(wbc[:, R_OWN : 2 * R_OWN], right[1][:, cols_of(k)], preferred_element_type=F32)
-        ip[k] = m.reshape(NN, ZR, WIDTH)
+        ip[k][...] = m.reshape(NN, ZR, WIDTHS[k])
         z_in[k] = [
-            send(ip.at[k, 3, pl.ds(0, ZR // 2)], iz1.at[k, 0], at(dz=1)),
-            send(ip.at[k, 3, pl.ds(ZR // 2, ZR // 2)], iz1.at[k, 1], at(dz=-1)),
+            send(ip[k].at[3, pl.ds(0, ZR // 2)], iz1[k].at[0], at(dz=1)),
+            send(ip[k].at[3, pl.ds(ZR // 2, ZR // 2)], iz1[k].at[1], at(dz=-1)),
         ]
 
     old = len(unsent)
@@ -300,15 +320,15 @@
 
     def text_merge(k):
         wait(*x_in[k])
-        tp[k, 1, 0 : XR // 2] += tx1[k, 0]
-        tp[k, 3, XR // 2 : XR] += tx1[k, 1]
-        x_in[k] = [send(tp.at[k, 1], tx2.at[k, 0], at(dx=1)), send(tp.at[k, 3], tx2.at[k, 1], at(dx=-1))]
+        tp[k][1, 0 : XR // 2] += tx1[k][0]
+        tp[k][3, XR // 2 : XR] += tx1[k][1]
+        x_in[k] = [send(tp[k].at[1], tx2[k].at[0], at(dx=1)), send(tp[k].at[3], tx2[k].at[1], at(dx=-1))]
 
     def image_merge(k):
         wait(*z_in[k])
-        ip[k, 1, 0 : ZR // 2] += iz1[k, 0]
-        ip[k, 2, 0 : ZR // 2] += iz1[k, 1]
-        z_in[k] = [send(ip.at[k, 1], iz2.at[k, 0], at(dz=1)), send(ip.at[k, 2], iz2.at[k, 1], at(dz=-1))]
+        ip[k][1, 0 : ZR // 2] += iz1[k][0]
+        ip[k][2, 0 : ZR // 2] += iz1[k][1]
+        z_in[k] = [send(ip[k].at[1], iz2[k].at[0], at(dz=1)), send(ip[k].at[2], iz2[k].at[1], at(dz=-1))]
 
     for k in range(NC):
         text_part(k)
@@ -328,21 +348,22 @@
     for k in range(NC):
         image_merge(k)
     old = len(unsent)
-    def far_send(k, entry):
-        return send(ip.at[k, 0, window(entry)], iw.at[k, entry - 1], at(dz=Z_FAR[entry]))
-
     for k in range(NC):
         over, other = (2, 3) if k % 2 == 0 else (3, 2)
         wait(*z_in[k])
-        ip[k, 0] += iz2[k, 0] + iz2[k, 1]
+        ip[k][0] += iz2[k][0] + iz2[k][1]
+        for e in (1, 2, 3):
+            pack(zb[k].at[e - 1], ip[k].at[0], ROWS * e)
         f_in[k] = [
-            send(ip.at[k, 0, window(1)], iw.at[k, 0], at(dz=Z_FAR[over])),
-            far_send(k, other),
+            send(zb[k].at[0], iw[k].at[0], at(dz=Z_FAR[over])),
+            send(zb[k].at[other - 1], iw[k].at[other - 1], at(dz=Z_FAR[other])),
         ]
         wait(*x_in[k])
-        tp[k, 0] += tx2[k, 0] + tx2[k, 1]
+        tp[k][0] += tx2[k][0] + tx2[k][1]
+        for j in range(1, NY):
+            pack(yb[k].at[j - 1], tp[k].at[0], ROWS * j)
         y_in[k] = send_all(
-            [(tp.at[k, 0, window(j)], ty.at[k, j - 1], at(dy=Y_OFF[j])) for j in (7, 5, 6, 3, 4, 1, 2)], ty.at[k]
+            [(yb[k].at[j - 1], ty[k].at[j - 1], at(dy=Y_OFF[j])) for j in (7, 5, 6, 3, 4, 1, 2)], ty[k]
         )
         if k == 0:
             stat_take(1, stat_got, 1)
@@ -350,25 +371,17 @@
     for k in range(NC):
         over = 2 if k % 2 == 0 else 3
         wait(f_in[k][0])
-        if over % 2 == 0:
-            fb[k, 0:ROWS] = ip[k, 0, 24:36] + iw[k, 0, PAD - ROWS : PAD]
-        else:
-            fb[k] = ip[k, 0, 32:48] + iw[k, 0]
-        f_in[k][0] = send(fb.at[k], iw.at[k, over - 1], at(dz=Z_FAR[over]))
+        zb[k][over - 1] += iw[k][0]
+        f_in[k][0] = send(zb[k].at[over - 1], iw[k].at[over - 1], at(dz=Z_FAR[over]))
     stat_take(2, stat_got, NY - 1)
     stat_got = stat_send(3, [at(dx=d) for d in (1, 2, 3)])
 
     wait_sent(old)
 
-    def total_of(own, ref, k, entries):
-        even, odd = own, None
-        for e in entries:
-            got = ref[k, e - 1]
-            if e % 2 == 0:
-                even = even + got
-            else:
-                odd = got if odd is None else odd + got
-        return even[0:ROWS] + odd[PAD - ROWS : PAD]
+    def total_of(i, own, got, entries):
+        for k in range(NC):
+            unpack(total.at[i], BEGINS[k], sum(got[k][e - 1] for e in entries))
+        return total[i] + jnp.concatenate([own[k][0, 0:ROWS] for k in range(NC)], axis=1)
 
     def back(ref, total, out_ref):
         u, inverse = unit(ref)
@@ -377,20 +390,27 @@
 
     for k in range(NC):
         wait(*f_in[k])
-    image_sums = [total_of(ip[k, 0, 0:PAD], iw, k, (2, 3)) for k in range(NC)]
+    image_sums = total_of(0, ip, iw, (2, 3))
     stat_take(3, stat_got, NX - 1)
     stat_got = stat_send(4, [at(dz=d) for d in (2, 1, -1)])
-    back(img_ref, jnp.concatenate(image_sums, axis=1), ig_ref)
+    back(img_ref, image_sums, ig_ref)
     for k in range(NC):
         wait(y_in[k])
     stat_take(4, stat_got, 3)
     stat_got = stat_send(5, [at(dc=1)])
-    text_sums = [total_of(tp[k, 0, 0:PAD], ty, k, range(1, NY)) for k in range(NC)]
-    back(txt_ref, jnp.concatenate(text_sums, axis=1), tg_ref)
+    back(txt_ref, total_of(1, tp, ty, range(1, NY)), tg_ref)
     stat_take(5, stat_got, 1)
     st_ref[0] = jnp.sum(stat[6, 0:8, :])
     st_ref[1] = jnp.sum(stat[6, 8:16, :])
     wait_sent(len(unsent))
+
+
+def per_part(*dims):
+    return tuple(pltpu.VMEM(dims + (w,), F32) for w in WIDTHS)
+
+
+def packed(n):
+    return tuple(pltpu.VMEM((n, 8, w + halves(w)[0]), F32) for w in WIDTHS)
 
 
 def shards(images, texts, log_scale, bias):
@@ -416,15 +436,17 @@
             pltpu.VMEM((NX * XR, 2 * L_OWN), BF16),
             pltpu.VMEM((NN * ZR, 2 * R_OWN), BF16),
             pltpu.VMEM((NX * XR, R_OWN), BF16),
-            pltpu.VMEM((NC, NX, XR, WIDTH), F32),
-            pltpu.VMEM((NC, 2, XR // 2, WIDTH), F32),
-            pltpu.VMEM((NC, 2, XR, WIDTH), F32),
-            pltpu.VMEM((NC, NY - 1, PAD, WIDTH), F32),
-            pltpu.VMEM((NC, NN, ZR, WIDTH), F32),
-            pltpu.VMEM((NC, 2, ZR // 2, WIDTH), F32),
-            pltpu.VMEM((NC, 2, ZR, WIDTH), F32),
-            pltpu.VMEM((NC, NF - 1, PAD, WIDTH), F32),
-            pltpu.VMEM((NC, PAD, WIDTH), F32),
+            per_part(NX, XR),
+            per_part(2, XR // 2),
+            per_part(2, XR),
+            packed(NY - 1),
+            packed(NY - 1),
+            per_part(NN, ZR),
+            per_part(2, ZR // 2),
+            per_part(2, ZR),
+            packed(NF - 1),
+            packed(NF - 1),
+            pltpu.VMEM((2, ROWS, D), F32),
             pltpu.VMEM((7, 16, 128), F32),
             pltpu.VMEM((6, NY - 1, 16, 128), F32),
             pltpu.SemaphoreType.DMA((2,)),

time: 87.6 us -> 85.1 us (0.971)
  Pallas kernels: 82.1 us -> 79.6 us
    pallas_call x1, Pallas kernels: 82.1 us -> 79.6 us  [shards(): pl.pallas_call(kernel, out_shape=(jax.ShapeDtypeStruct((ROWS, D), F32), j...]
where the time goes in v5:
time: 85.1 us; the launch traced here: 84.9 us
  Pallas kernels  79.6 us (94%)
  local copies, waits for them, and re-layouts  3.31 us (4%)
  between operations  1.94 us (2%)
    pallas_call x1, Pallas kernels, shards(): pl.pallas_call(kernel, out_shape=(jax.ShapeDtypeStruct((ROWS, D), F32), j...  79.6 us
    unnamed x7, local copies, waits for them, and re-layouts  3.31 us

profile of v5, /device:TPU:1, one launch (start us, length us, event | category | flops | bytes accessed | tf_op | source)
XLA Modules:
  0.0 84.9 jit_solution(7223843407925171967)
XLA Ops:
  1.9 0.0 copy-start
  1.9 0.8 copy-done
  2.7 0.0 copy-start.1
  2.7 0.8 copy-done.1
  3.5 79.6 %pair_gradients.1 = (f32[12,1152]{1,0:T(8,128)S(1)}, f32[12,1152]{1,0:T(8,128)S(1)}, f32[2]{0:T(128)S(1)}) custom-call(bf16[12,1152]{1,0:T(8,128)(2,1)S(1)} %copy-done, bf16[12,1152]{1,0:T(8,128)(2,1)S(1)} %copy-done.1, f32[1]{0:T(128)S(6)} %copy.10.ls_ref, f32[1]{0:T(128)S(6)} %copy.11.bias_ref), custom_call_target="tpu_custom_call" | custom-call | flops 1811939328 | bytes 1048576 | tf_op jit(solution)/shard_map/pair_gradients/pallas_call | solution.py:419
  83.1 0.6 copy.12
  83.7 0.6 copy.13
  84.3 0.5 copy.14
Async XLA Ops:
  1.9 0.8 copy-start
  2.7 0.8 copy-start.1

commit v6 on v5

--- a/solution.py
+++ b/solution.py
@@ -16,8 +16,8 @@
 NX, NY, NN, NF = 4, 8, 4, 4
 L_OWN, R_OWN = NN * NF * PAD, NX * NY * PAD
 XR, ZR = NY * ROWS, NF * ROWS
-WIDTHS = (256, 512, 384)
-BEGINS = (0, 256, 768)
+WIDTHS = (512, 384, 256)
+BEGINS = (0, 512, 896)
 NC = len(WIDTHS)
 SPLIT = 896
 MESH = pl.DeviceIdType.MESH
@@ -295,15 +295,21 @@
     def cols_of(k):
         return pl.ds(BEGINS[k], WIDTHS[k])
 
-    x_in, z_in = {}, {}
+    x_in, z_in, x_out, z_out = {}, {}, {}, {}
+    x_lo, x_hi = pl.ds(0, XR // 2), pl.ds(XR // 2, XR // 2)
+    z_lo, z_hi = pl.ds(0, ZR // 2), pl.ds(ZR // 2, ZR // 2)
 
     def text_part(k):
         t = jnp.dot(wtc[:, 0:L_OWN], left[0][:, cols_of(k)], preferred_element_type=F32)
         t += jnp.dot(wtc[:, L_OWN : 2 * L_OWN], left[1][:, cols_of(k)], preferred_element_type=F32)
         tp[k][...] = t.reshape(NX, XR, WIDTHS[k])
         x_in[k] = [
-            send(tp[k].at[2, pl.ds(0, XR // 2)], tx1[k].at[0], at(dx=1)),
-            send(tp[k].at[2, pl.ds(XR // 2, XR // 2)], tx1[k].at[1], at(dx=-1)),
+            send(tp[k].at[2, x_lo], tx1[k].at[0], at(dx=1)),
+            send(tp[k].at[2, x_hi], tx1[k].at[1], at(dx=-1)),
+        ]
+        x_out[k] = [
+            send(tp[k].at[1, x_hi], tx2[k].at[0, x_hi], at(dx=1)),
+            send(tp[k].at[3, x_lo], tx2[k].at[1, x_lo], at(dx=-1)),
         ]
 
     def image_part(k):
@@ -311,8 +317,12 @@
         m += jnp.dot(wbc[:, R_OWN : 2 * R_OWN], right[1][:, cols_of(k)], preferred_element_type=F32)
         ip[k][...] = m.reshape(NN, ZR, WIDTHS[k])
         z_in[k] = [
-            send(ip[k].at[3, pl.ds(0, ZR // 2)], iz1[k].at[0], at(dz=1)),
-            send(ip[k].at[3, pl.ds(ZR // 2, ZR // 2)], iz1[k].at[1], at(dz=-1)),
+            send(ip[k].at[3, z_lo], iz1[k].at[0], at(dz=1)),
+            send(ip[k].at[3, z_hi], iz1[k].at[1], at(dz=-1)),
+        ]
+        z_out[k] = [
+            send(ip[k].at[1, z_hi], iz2[k].at[0, z_hi], at(dz=1)),
+            send(ip[k].at[2, z_hi], iz2[k].at[1, z_hi], at(dz=-1)),
         ]
 
     old = len(unsent)
@@ -322,13 +332,19 @@
         wait(*x_in[k])
         tp[k][1, 0 : XR // 2] += tx1[k][0]
         tp[k][3, XR // 2 : XR] += tx1[k][1]
-        x_in[k] = [send(tp[k].at[1], tx2[k].at[0], at(dx=1)), send(tp[k].at[3], tx2[k].at[1], at(dx=-1))]
+        x_out[k] += [
+            send(tp[k].at[1, x_lo], tx2[k].at[0, x_lo], at(dx=1)),
+            send(tp[k].at[3, x_hi], tx2[k].at[1, x_hi], at(dx=-1)),
+        ]
 
     def image_merge(k):
         wait(*z_in[k])
         ip[k][1, 0 : ZR // 2] += iz1[k][0]
         ip[k][2, 0 : ZR // 2] += iz1[k][1]
-        z_in[k] = [send(ip[k].at[1], iz2[k].at[0], at(dz=1)), send(ip[k].at[2], iz2[k].at[1], at(dz=-1))]
+        z_out[k] += [
+            send(ip[k].at[1, z_lo], iz2[k].at[0, z_lo], at(dz=1)),
+            send(ip[k].at[2, z_lo], iz2[k].at[1, z_lo], at(dz=-1)),
+        ]
 
     for k in range(NC):
         text_part(k)
@@ -338,19 +354,23 @@
     wait(*shared_r)
     image_weights(1)
     wbc[...] = jnp.dot(sel[0 : NN * ZR, 0:L_OWN], wb[...], preferred_element_type=F32).astype(BF16)
-    for k in range(NC):
-        image_part(k)
-        text_merge(k)
-        if k == 0:
-            stat_take(0, stat_got, 2)
-            stat_got = send(stat_in.at[0, 0], stat_in.at[1, 0], at(dz=4))
+    image_part(0)
+    text_merge(0)
+    image_part(1)
+    image_part(2)
+    stat_take(0, stat_got, 2)
+    stat_got = send(stat_in.at[0, 0], stat_in.at[1, 0], at(dz=4))
+    image_merge(0)
+    text_merge(1)
+    image_merge(1)
     wait_sent(old)
-    for k in range(NC):
-        image_merge(k)
+    text_merge(2)
+    image_merge(2)
     old = len(unsent)
-    for k in range(NC):
+
+    def image_far(k):
         over, other = (2, 3) if k % 2 == 0 else (3, 2)
-        wait(*z_in[k])
+        wait(*z_out[k])
         ip[k][0] += iz2[k][0] + iz2[k][1]
         for e in (1, 2, 3):
             pack(zb[k].at[e - 1], ip[k].at[0], ROWS * e)
@@ -358,21 +378,33 @@
             send(zb[k].at[0], iw[k].at[0], at(dz=Z_FAR[over])),
             send(zb[k].at[other - 1], iw[k].at[other - 1], at(dz=Z_FAR[other])),
         ]
-        wait(*x_in[k])
+
+    def image_over(k):
+        over = 2 if k % 2 == 0 else 3
+        wait(f_in[k][0])
+        zb[k][over - 1] += iw[k][0]
+        f_in[k][0] = send(zb[k].at[over - 1], iw[k].at[over - 1], at(dz=Z_FAR[over]))
+
+    def text_far(k):
+        wait(*x_out[k])
         tp[k][0] += tx2[k][0] + tx2[k][1]
         for j in range(1, NY):
             pack(yb[k].at[j - 1], tp[k].at[0], ROWS * j)
         y_in[k] = send_all(
             [(yb[k].at[j - 1], ty[k].at[j - 1], at(dy=Y_OFF[j])) for j in (7, 5, 6, 3, 4, 1, 2)], ty[k]
         )
-        if k == 0:
-            stat_take(1, stat_got, 1)
-            stat_got = stat_send(2, [at(dy=d) for d in Y_OFF[1:]])
-    for k in range(NC):
-        over = 2 if k % 2 == 0 else 3
-        wait(f_in[k][0])
-        zb[k][over - 1] += iw[k][0]
-        f_in[k][0] = send(zb[k].at[over - 1], iw[k].at[over - 1], at(dz=Z_FAR[over]))
+
+    image_far(0)
+    text_far(0)
+    stat_take(1, stat_got, 1)
+    stat_got = stat_send(2, [at(dy=d) for d in Y_OFF[1:]])
+    image_far(1)
+    image_far(2)
+    text_far(1)
+    image_over(0)
+    image_over(1)
+    text_far(2)
+    image_over(2)
     stat_take(2, stat_got, NY - 1)
     stat_got = stat_send(3, [at(dx=d) for d in (1, 2, 3)])
 

time: 85.1 us -> 86 us (1.011)
  no operation moved by 1% of the time
where the time goes in v6:
time: 86 us; the launch traced here: 85.7 us
  Pallas kernels  80.4 us (93%)
  local copies, waits for them, and re-layouts  3.31 us (4%)
  between operations  1.94 us (2%)
    pallas_call x1, Pallas kernels, shards(): pl.pallas_call(kernel, out_shape=(jax.ShapeDtypeStruct((ROWS, D), F32), j...  80.4 us
    unnamed x7, local copies, waits for them, and re-layouts  3.31 us

profile of v6, /device:TPU:1, one launch (start us, length us, event | category | flops | bytes accessed | tf_op | source)
XLA Modules:
  0.0 85.7 jit_solution(8363699181752030039)
XLA Ops:
  1.9 0.0 copy-start
  1.9 0.8 copy-done
  2.7 0.0 copy-start.1
  2.7 0.8 copy-done.1
  3.5 80.4 %pair_gradients.1 = (f32[12,1152]{1,0:T(8,128)S(1)}, f32[12,1152]{1,0:T(8,128)S(1)}, f32[2]{0:T(128)S(1)}) custom-call(bf16[12,1152]{1,0:T(8,128)(2,1)S(1)} %copy-done, bf16[12,1152]{1,0:T(8,128)(2,1)S(1)} %copy-done.1, f32[1]{0:T(128)S(6)} %copy.10.ls_ref, f32[1]{0:T(128)S(6)} %copy.11.bias_ref), custom_call_target="tpu_custom_call" | custom-call | flops 1811939328 | bytes 1048576 | tf_op jit(solution)/shard_map/pair_gradients/pallas_call | solution.py:451
  83.9 0.6 copy.12
  84.5 0.6 copy.13
  85.2 0.5 copy.14
Async XLA Ops:
  1.9 0.8 copy-start
  2.7 0.8 copy-start.1

commit v7 on v6

--- a/solution.py
+++ b/solution.py
@@ -207,12 +207,11 @@
         wait(x3[s])
         if s == 2:
             wait(x0[2], x1[2], x2[2])
-        shared_r.append(send(rall.at[0, s], rall.at[1, s], at(dc=1)))
-    for s in (2, 1):
-        wait(n2[s])
-        shared_l.append(send(lall.at[0, s], lall.at[1, s], at(dc=1)))
-    wait(*last)
-    shared_l.append(send(lall.at[0, 3], lall.at[1, 3], at(dc=1)))
+    far = pl.ds(1, NX - 1)
+    shared_r.append(send(rall.at[0, far], rall.at[1, far], at(dc=1)))
+    wait(n2[1], n2[2], *last)
+    near = pl.ds(1, NN - 1)
+    shared_l.append(send(lall.at[0, near], lall.at[1, near], at(dc=1)))
 
     scale = jnp.exp(jnp.full((1, 1), ls_ref[0], F32))
     shift = jnp.full((1, 1), bias_ref[0], F32)
@@ -307,10 +306,6 @@
             send(tp[k].at[2, x_lo], tx1[k].at[0], at(dx=1)),
             send(tp[k].at[2, x_hi], tx1[k].at[1], at(dx=-1)),
         ]
-        x_out[k] = [
-            send(tp[k].at[1, x_hi], tx2[k].at[0, x_hi], at(dx=1)),
-            send(tp[k].at[3, x_lo], tx2[k].at[1, x_lo], at(dx=-1)),
-        ]
 
     def image_part(k):
         m = jnp.dot(wbc[:, 0:R_OWN], right[0][:, cols_of(k)], preferred_element_type=F32)
@@ -320,10 +315,6 @@
             send(ip[k].at[3, z_lo], iz1[k].at[0], at(dz=1)),
             send(ip[k].at[3, z_hi], iz1[k].at[1], at(dz=-1)),
         ]
-        z_out[k] = [
-            send(ip[k].at[1, z_hi], iz2[k].at[0, z_hi], at(dz=1)),
-            send(ip[k].at[2, z_hi], iz2[k].at[1, z_hi], at(dz=-1)),
-        ]
 
     old = len(unsent)
     f_in, y_in = {}, {}
@@ -332,19 +323,13 @@
         wait(*x_in[k])
         tp[k][1, 0 : XR // 2] += tx1[k][0]
         tp[k][3, XR // 2 : XR] += tx1[k][1]
-        x_out[k] += [
-            send(tp[k].at[1, x_lo], tx2[k].at[0, x_lo], at(dx=1)),
-            send(tp[k].at[3, x_hi], tx2[k].at[1, x_hi], at(dx=-1)),
-        ]
+        x_out[k] = [send(tp[k].at[1], tx2[k].at[0], at(dx=1)), send(tp[k].at[3], tx2[k].at[1], at(dx=-1))]
 
     def image_merge(k):
         wait(*z_in[k])
         ip[k][1, 0 : ZR // 2] += iz1[k][0]
         ip[k][2, 0 : ZR // 2] += iz1[k][1]
-        z_out[k] += [
-            send(ip[k].at[1, z_lo], iz2[k].at[0, z_lo], at(dz=1)),
-            send(ip[k].at[2, z_lo], iz2[k].at[1, z_lo], at(dz=-1)),
-        ]
+        z_out[k] = [send(ip[k].at[1], iz2[k].at[0], at(dz=1)), send(ip[k].at[2], iz2[k].at[1], at(dz=-1))]
 
     for k in range(NC):
         text_part(k)

time: 86 us -> 84 us (0.977)
  Pallas kernels: 80.4 us -> 78.5 us
    pallas_call x1, Pallas kernels: 80.4 us -> 78.5 us  [shards(): pl.pallas_call(kernel, out_shape=(jax.ShapeDtypeStruct((ROWS, D), F32), j...]
where the time goes in v7:
time: 84 us; the launch traced here: 83.7 us
  Pallas kernels  78.5 us (93%)
  local copies, waits for them, and re-layouts  3.31 us (4%)
  between operations  1.94 us (2%)
    pallas_call x1, Pallas kernels, shards(): pl.pallas_call(kernel, out_shape=(jax.ShapeDtypeStruct((ROWS, D), F32), j...  78.5 us
    unnamed x7, local copies, waits for them, and re-layouts  3.31 us

profile of v7, /device:TPU:1, one launch (start us, length us, event | category | flops | bytes accessed | tf_op | source)
XLA Modules:
  0.0 83.7 jit_solution(3021764198055516187)
XLA Ops:
  1.9 0.0 copy-start
  1.9 0.8 copy-done
  2.7 0.0 copy-start.1
  2.7 0.8 copy-done.1
  3.5 78.5 %pair_gradients.1 = (f32[12,1152]{1,0:T(8,128)S(1)}, f32[12,1152]{1,0:T(8,128)S(1)}, f32[2]{0:T(128)S(1)}) custom-call(bf16[12,1152]{1,0:T(8,128)(2,1)S(1)} %copy-done, bf16[12,1152]{1,0:T(8,128)(2,1)S(1)} %copy-done.1, f32[1]{0:T(128)S(6)} %copy.10.ls_ref, f32[1]{0:T(128)S(6)} %copy.11.bias_ref), custom_call_target="tpu_custom_call" | custom-call | flops 1811939328 | bytes 1048576 | tf_op jit(solution)/shard_map/pair_gradients/pallas_call | solution.py:436
  81.9 0.6 copy.12
  82.6 0.6 copy.13
  83.2 0.5 copy.14
Async XLA Ops:
  1.9 0.8 copy-start
  2.7 0.8 copy-start.1

commit v8 on v7

--- a/solution.py
+++ b/solution.py
@@ -132,9 +132,9 @@
 
     z_below = send(img_own.at[0], img_own.at[3], at(dz=4))
     z_above = send(img_own.at[0], img_own.at[2], at(dz=-4))
-    x_rest = send_all(
-        [(rall.at[0, 0, 0, :, rest], rall.at[0, X - d, 0, :, rest], at(dx=d)) for d in (2, 1, 3)],
-        rall.at[0, pl.ds(1, NX - 1), 0, :, rest],
+    x_own = send_all(
+        [(txt_own.at[0], rall.at[0, X - d, 0], at(dx=d)) for d in (2, 1, 3)],
+        rall.at[0, pl.ds(1, NX - 1), 0],
     )
     y_far = y_first(7, 5, 6)
     y_two, y_one = y_first(3, 4), y_first(1, 2)
@@ -167,8 +167,7 @@
         return send(lall.at[0, frm, entry], lall.at[0, 3, to], at(dz=-Z_NEAR[frm]))
 
     n0 = n_send(0, 1)
-    x0 = x_send(0, 1)
-    wait(x_rest)
+    wait(x_own)
     near = [(j, slot(Y_OFF, Y, -Y_OFF[j])) for j in (7, 5, 6, 3, 4, 1, 2)]
     y_rest = send_all(
         [(rall.at[0, :, 0, :, rest], rall.at[0, :, t, :, rest], at(dy=Y_OFF[j])) for j, t in near],
@@ -176,7 +175,6 @@
     )
     wait(y_one)
     x1 = x_send(1, 3)
-    x_relay(x0, 3, 0, 1)
     wait(y_two)
     x2 = x_send(3, 5)
     wait(z_below, z_above)
@@ -200,13 +198,13 @@
     wait(z_eight)
     n2 = n_send(1, 2)
     shared_l = [send(lall.at[0, 0], lall.at[1, 0], at(dc=1))]
-    wait(x0[1], x1[3], x2[1])
+    wait(x1[3], x2[1])
     wait(y_rest)
     shared_r = [send(rall.at[0, 0], rall.at[1, 0], at(dc=1))]
     for s in (3, 1, 2):
         wait(x3[s])
         if s == 2:
-            wait(x0[2], x1[2], x2[2])
+            wait(x1[2], x2[2])
     far = pl.ds(1, NX - 1)
     shared_r.append(send(rall.at[0, far], rall.at[1, far], at(dc=1)))
     wait(n2[1], n2[2], *last)
@@ -388,10 +386,10 @@
     text_far(1)
     image_over(0)
     image_over(1)
+    stat_take(2, stat_got, NY - 1)
+    stat_got = stat_send(3, [at(dx=d) for d in (1, 2, 3)])
     text_far(2)
     image_over(2)
-    stat_take(2, stat_got, NY - 1)
-    stat_got = stat_send(3, [at(dx=d) for d in (1, 2, 3)])
 
     wait_sent(old)
 
@@ -405,16 +403,16 @@
         grad = scale * total
         out_ref[...] = (grad - u * jnp.sum(u * grad, axis=1, keepdims=True)) * inverse
 
+    stat_take(3, stat_got, NX - 1)
+    stat_got = stat_send(4, [at(dz=d) for d in (2, 1, -1)])
     for k in range(NC):
         wait(*f_in[k])
     image_sums = total_of(0, ip, iw, (2, 3))
-    stat_take(3, stat_got, NX - 1)
-    stat_got = stat_send(4, [at(dz=d) for d in (2, 1, -1)])
+    stat_take(4, stat_got, 3)
+    stat_got = stat_send(5, [at(dc=1)])
     back(img_ref, image_sums, ig_ref)
     for k in range(NC):
         wait(y_in[k])
-    stat_take(4, stat_got, 3)
-    stat_got = stat_send(5, [at(dc=1)])
     back(txt_ref, total_of(1, tp, ty, range(1, NY)), tg_ref)
     stat_take(5, stat_got, 1)
     st_ref[0] = jnp.sum(stat[6, 0:8, :])

time: 84 us -> 83.9 us (level)
  no operation moved by 1% of the time
where the time goes in v8:
time: 83.9 us; the launch traced here: 83.6 us
  Pallas kernels  78.4 us (93%)
  local copies, waits for them, and re-layouts  3.31 us (4%)
  between operations  1.94 us (2%)
    pallas_call x1, Pallas kernels, shards(): pl.pallas_call(kernel, out_shape=(jax.ShapeDtypeStruct((ROWS, D), F32), j...  78.4 us
    unnamed x7, local copies, waits for them, and re-layouts  3.31 us

profile of v8, /device:TPU:1, one launch (start us, length us, event | category | flops | bytes accessed | tf_op | source)
XLA Modules:
  0.0 83.6 jit_solution(2163988240528417126)
XLA Ops:
  1.9 0.0 copy-start
  1.9 0.8 copy-done
  2.7 0.0 copy-start.1
  2.7 0.8 copy-done.1
  3.5 78.4 %pair_gradients.1 = (f32[12,1152]{1,0:T(8,128)S(1)}, f32[12,1152]{1,0:T(8,128)S(1)}, f32[2]{0:T(128)S(1)}) custom-call(bf16[12,1152]{1,0:T(8,128)(2,1)S(1)} %copy-done, bf16[12,1152]{1,0:T(8,128)(2,1)S(1)} %copy-done.1, f32[1]{0:T(128)S(6)} %copy.10.ls_ref, f32[1]{0:T(128)S(6)} %copy.11.bias_ref), custom_call_target="tpu_custom_call" | custom-call | flops 1811939328 | bytes 1048576 | tf_op jit(solution)/shard_map/pair_gradients/pallas_call | solution.py:434
  81.9 0.6 copy.12
  82.5 0.6 copy.13
  83.1 0.5 copy.14
Async XLA Ops:
  1.9 0.8 copy-start
  2.7 0.8 copy-start.1
